TPU v7x, 128 devices: a whole 4x4x4 slice. The times are simulated.
128 devices in a mesh: dp: 16 (over x, y_lo, core), tensor: 8 (over y_hi, z).
Axes of the slice: x: 4, y: 4 (y_hi: 2, y_lo: 2; y = y_hi * 2 + y_lo), z: 4, core: 2. Of those that a mesh axis runs over, the one named last changes fastest.
Arguments:
- tokens: bfloat16 [16384, 1024], P(('dp', 'tensor')), may hold values from -6 to 6
- input_proj: bfloat16 [3, 1024, 1024], P(None, 'dp', 'tensor'), may hold values from -0.25 to 0.25
- output_proj: bfloat16 [1024, 1024], P('tensor', 'dp'), may hold values from -0.75 to 0.75
- expand_proj: bfloat16 [1024, 4096], P('dp', 'tensor'), may hold values from -0.1875 to 0.1875
- contract_proj: bfloat16 [4096, 1024], P('tensor', 'dp'), may hold values from -0.09375 to 0.09375
- head_bias: bfloat16 [2, 8, 128], P(None, 'tensor', 'dp'), may hold values from -3 to 3
- hidden_bias: bfloat16 [8, 512], P('tensor', 'dp'), may hold values from -3 to 3
- norm_gains: bfloat16 [2, 1024], P(None, 'dp'), may hold values from 0.25 to 1.75
- offsets: bfloat16 [4, 1024], P(None, 'dp'), may hold values from -2 to 2
- cotangent: bfloat16 [16384, 1024], P(('dp', 'tensor')), may hold values from -24 to 24
Outputs:
- output: bfloat16 [16384, 1024], P(('dp', 'tensor'))
- grad_tokens: float32 [16384, 1024], P(('dp', 'tensor'))
- grad_input_proj: float32 [3, 1024, 1024], P(None, 'dp', 'tensor')
- grad_output_proj: float32 [1024, 1024], P('tensor', 'dp')
- grad_expand_proj: float32 [1024, 4096], P('dp', 'tensor')
- grad_contract_proj: float32 [4096, 1024], P('tensor', 'dp')
- grad_head_bias: float32 [2, 8, 128], P(None, 'tensor', 'dp')
- grad_hidden_bias: float32 [8, 512], P('tensor', 'dp')
- grad_norm_gains: float32 [2, 1024], P(None, 'dp')
- grad_offsets: float32 [4, 1024], P(None, 'dp')
All inputs are finite; a program needn't handle non-finite values.
Results may differ from a plain program's by a relative error of at most 0.03.
Values may be sent and summed in bfloat16 or wider, within the bound.
A program may use at most 128 MiB of HBM per device.

v0:
```python
import jax
import jax.numpy as jnp
from jax import lax
from jax.sharding import Mesh
from jax.sharding import PartitionSpec as P

HD = 64
SEQ_LEN = 1024
DP = ("dp_0", "dp_1", "dp_2")
DP_TENSOR = ("dp_0", "dp_1", "dp_2", "tensor")


EPSILON = 1e-05
MASKED = -1000000000.0
GELU_COEF = 0.7978845608028654
CUBIC = 0.044715


def in_one_piece(arrays, axis, dim, along):
    widths = [a.shape[along] for a in arrays]
    both = jnp.concatenate(arrays, axis=along)
    whole = lax.all_gather(both, axis, axis=dim, tiled=True)
    return tuple(jnp.split(whole, [sum(widths[:k]) for k in range(1, len(widths))], axis=along))


def sent_to_all(value, axis):
    devices = lax.axis_size(axis)
    return lax.all_to_all(
        jnp.broadcast_to(value[None], (devices, *value.shape)), axis, 0, 0, tiled=True
    )


def laid_out(tiles, dim):
    tiles = jnp.moveaxis(tiles, 0, dim)
    lengths = tiles.shape
    return tiles.reshape(*lengths[:dim], lengths[dim] * lengths[dim + 1], *lengths[dim + 2 :])


def collect(value, axis, dim):
    tiles = sent_to_all(value, axis)
    return laid_out(tiles, dim)


def of_everyone(value, axis):
    return sent_to_all(value, axis).sum(axis=0)


def packed_total(arrays, axis):
    flat, at, outs = (jnp.concatenate([a.reshape(-1) for a in arrays]), 0, [])
    total = of_everyone(flat, axis)
    for a in arrays:
        outs.append(total[at : at + a.size].reshape(a.shape))
        at += a.size
    return tuple(outs)


def in_blocks(value, dim, devices):
    before, after = (value.shape[:dim], value.shape[dim + 1 :])
    return jnp.moveaxis(value.reshape(*before, devices, -1, *after), dim, 0)


def sent_and_summed(value, axis, dim):
    devices = lax.axis_size(axis)
    tiles = lax.all_to_all(in_blocks(value, dim, devices), axis, 0, 0, tiled=True)
    return jnp.sum(tiles.astype(jnp.float32), axis=0)


def summed_rows_2(value, axes, dim):
    far, near = axes
    own = sent_and_summed(in_blocks(value, dim, lax.axis_size(far)), near, dim + 1)
    return jnp.sum(
        lax.all_to_all(own.astype(jnp.bfloat16), far, 0, 0, tiled=True).astype(jnp.float32), axis=0
    )


def sent_together(arrays, axis, dim, along):
    widths = [a.shape[along] for a in arrays]
    both = jnp.concatenate(arrays, axis=along)
    whole = summed_rows_2(both, axis, dim)
    return tuple(jnp.split(whole, [sum(widths[:k]) for k in range(1, len(widths))], axis=along))


def gelu_tanh(preact):
    return 0.5 * preact * (1.0 + jnp.tanh(GELU_COEF * (preact + CUBIC * preact * preact * preact)))


def norm_forward(row_values, norm_gain, offset):
    centre = jnp.mean(row_values, axis=-1, keepdims=True)
    shifted = row_values - centre
    spread = jnp.mean(shifted * shifted, axis=-1, keepdims=True)
    inverse = lax.rsqrt(spread + EPSILON)
    normed = shifted * inverse
    return (normed * norm_gain + offset, normed, inverse)


def norm_backward(grad_rows, normed, inverse, norm_gain):
    scaled = grad_rows * norm_gain
    first_mean = jnp.mean(scaled, axis=-1, keepdims=True)
    second_mean = jnp.mean(scaled * normed, axis=-1, keepdims=True)
    return inverse * (scaled - first_mean - normed * second_mean)


def block_scores(query_block, key_rows, first_row, finish, score_scale):
    block_rows = query_block.shape[0]
    scores = (
        jnp.einsum(
            "qhd,khd->hqk", query_block, key_rows[:finish], preferred_element_type=jnp.float32
        )
        * score_scale
    )
    row_index = lax.broadcasted_iota(jnp.int32, (block_rows, finish), 0) + first_row
    col_index = lax.broadcasted_iota(jnp.int32, (block_rows, finish), 1)
    return jnp.where((row_index >= col_index)[None], scores, MASKED)


def attend_forward(queries, key_rows, values, block_rows, score_scale):
    outputs = []
    log_sums = []
    for first_row in range(0, queries.shape[0], block_rows):
        finish = first_row + block_rows
        scores = block_scores(queries[first_row:finish], key_rows, first_row, finish, score_scale)
        row_peak = jnp.max(scores, axis=-1, keepdims=True)
        exponent = jnp.exp(scores - row_peak)
        row_total = jnp.sum(exponent, axis=-1, keepdims=True)
        attn_probs = (exponent / row_total).astype(jnp.bfloat16)
        outputs.append(
            jnp.einsum(
                "hqk,khd->qhd", attn_probs, values[:finish], preferred_element_type=jnp.float32
            )
        )
        log_sums.append(row_peak + jnp.log(row_total))
    return (jnp.concatenate(outputs, axis=0), jnp.concatenate(log_sums, axis=1))


def attend_backward(queries, key_rows, values, grad_attended, log_sums, block_rows, score_scale):
    grad_keys = jnp.zeros(key_rows.shape, jnp.float32)
    grad_values = jnp.zeros(values.shape, jnp.float32)
    query_grads = []
    for first_row in range(0, queries.shape[0], block_rows):
        finish = first_row + block_rows
        query_block = queries[first_row:finish]
        grad_block = grad_attended[first_row:finish]
        scores = block_scores(query_block, key_rows, first_row, finish, score_scale)
        soft_rows = jnp.exp(scores - log_sums[:, first_row:finish])
        grad_soft = jnp.einsum(
            "qhd,khd->hqk", grad_block, values[:finish], preferred_element_type=jnp.float32
        )
        row_dot = jnp.sum(soft_rows * grad_soft, axis=-1, keepdims=True)
        grad_scores = (soft_rows * (grad_soft - row_dot)).astype(jnp.bfloat16)
        query_grads.append(
            jnp.einsum(
                "hqk,khd->qhd", grad_scores, key_rows[:finish], preferred_element_type=jnp.float32
            )
            * score_scale
        )
        key_part = (
            jnp.einsum("hqk,qhd->khd", grad_scores, query_block, preferred_element_type=jnp.float32)
            * score_scale
        )
        grad_keys = grad_keys.at[:finish].add(key_part)
        value_part = jnp.einsum(
            "hqk,qhd->khd",
            soft_rows.astype(jnp.bfloat16),
            grad_block,
            preferred_element_type=jnp.float32,
        )
        grad_values = grad_values.at[:finish].add(value_part)
    grad_queries = jnp.concatenate(query_grads, axis=0)
    return (
        grad_queries.astype(jnp.bfloat16),
        grad_keys.astype(jnp.bfloat16),
        grad_values.astype(jnp.bfloat16),
    )


def per_device(
    tokens,
    input_proj,
    output_proj,
    expand_proj,
    contract_proj,
    head_bias,
    hidden_bias,
    norm_gains,
    offsets,
    cotangent,
):
    local_rows = tokens.shape[0]
    tensor_count = lax.axis_size("tensor")
    group_rows = local_rows * tensor_count
    (
        full_input,
        full_output,
        full_expand,
        full_contract,
        full_head_bias,
        full_hidden_bias,
        full_gains,
        full_offsets,
    ) = (
        lax.all_gather(input_proj, DP, axis=1, tiled=True),
        lax.all_gather(output_proj, DP, axis=1, tiled=True),
        lax.all_gather(expand_proj, DP, axis=0, tiled=True),
        lax.all_gather(contract_proj, DP, axis=1, tiled=True),
        lax.all_gather(head_bias, DP, axis=2, tiled=True),
        lax.all_gather(hidden_bias, DP, axis=1, tiled=True),
        *in_one_piece((norm_gains, offsets), DP, 1, 0),
    )
    gain_vals = full_gains.astype(jnp.float32)
    offset_vals = full_offsets.astype(jnp.float32)
    token_vals = tokens.astype(jnp.float32)
    first_norm, normed_one, inverse_one = norm_forward(token_vals, gain_vals[0], offset_vals[0])
    norm_rows = collect(first_norm.astype(jnp.bfloat16), "tensor", 0)
    bias_three = jnp.stack(
        [full_head_bias[0, 0], jnp.zeros_like(full_head_bias[0, 0]), full_head_bias[1, 0]]
    ).astype(jnp.float32)
    projected = (
        jnp.einsum("td,idc->itc", norm_rows, full_input, preferred_element_type=jnp.float32)
        + bias_three[:, None, :]
    )
    projected = projected.astype(jnp.bfloat16)
    col_count = projected.shape[2]
    head_count = col_count // HD
    seq_count = group_rows // SEQ_LEN
    block_rows = min(512, SEQ_LEN)
    score_scale = HD ** (-0.5)
    shaped = projected.reshape(3, seq_count, SEQ_LEN, head_count, HD)
    seq_index = 0
    result, log_sum = attend_forward(
        shaped[0, seq_index], shaped[1, seq_index], shaped[2, seq_index], block_rows, score_scale
    )
    sums_list = [log_sum]
    attended = result.astype(jnp.bfloat16).reshape(group_rows, col_count)
    piece = attended
    branch = (
        lax.psum_scatter(
            jnp.dot(piece, full_output, preferred_element_type=jnp.float32),
            "tensor",
            scatter_dimension=0,
            tiled=True,
        )
        + offset_vals[1]
    )
    resid = token_vals + branch
    second_norm, normed_two, inverse_two = norm_forward(resid, gain_vals[1], offset_vals[2])
    second_low = second_norm.astype(jnp.bfloat16)
    mlp_rows = collect(second_low, "tensor", 0)
    preact = jnp.dot(
        mlp_rows, full_expand, preferred_element_type=jnp.float32
    ) + full_hidden_bias.astype(jnp.float32).reshape(-1)
    hidden = gelu_tanh(preact).astype(jnp.bfloat16)
    piece = hidden
    output_vals = (
        resid
        + lax.psum_scatter(
            jnp.dot(piece, full_contract, preferred_element_type=jnp.float32).astype(jnp.bfloat16),
            "tensor",
            scatter_dimension=0,
            tiled=True,
        ).astype(jnp.float32)
        + offset_vals[3]
    )
    output = output_vals.astype(jnp.bfloat16)
    back_input, back_output, back_expand, back_contract = (
        full_input,
        full_output,
        full_expand,
        full_contract,
    )
    _, gelu_pull = jax.vjp(gelu_tanh, preact)
    grad_rows = collect(cotangent, "tensor", 0)
    grad_contract = jnp.einsum("th,td->hd", hidden, grad_rows, preferred_element_type=jnp.float32)
    grad_hidden = jnp.einsum(
        "td,hd->th", grad_rows, back_contract, preferred_element_type=jnp.float32
    )
    grad_preact = gelu_pull(grad_hidden)[0].astype(jnp.bfloat16)
    grad_hidden_bias = jnp.sum(grad_preact, axis=0, dtype=jnp.float32)[None]
    grad_expand = jnp.einsum("td,th->dh", mlp_rows, grad_preact, preferred_element_type=jnp.float32)
    piece = grad_preact
    grad_second = lax.psum_scatter(
        jnp.einsum("th,dh->td", piece, back_expand, preferred_element_type=jnp.float32).astype(
            jnp.bfloat16
        ),
        "tensor",
        scatter_dimension=0,
        tiled=True,
    ).astype(jnp.float32)
    grad_resid = cotangent.astype(jnp.float32) + norm_backward(
        grad_second, normed_two, inverse_two, gain_vals[1]
    )
    grad_branch = grad_resid.astype(jnp.bfloat16)
    branch_rows = collect(grad_branch, "tensor", 0)
    grad_output = jnp.einsum("tc,td->cd", attended, branch_rows, preferred_element_type=jnp.float32)
    grad_attended = jnp.einsum(
        "td,cd->tc", branch_rows, back_output, preferred_element_type=jnp.float32
    ).astype(jnp.bfloat16)
    grad_shaped = grad_attended.reshape(seq_count, SEQ_LEN, head_count, HD)
    seq_index = 0
    grad_q_seq, grad_k_seq, grad_v_seq = attend_backward(
        shaped[0, seq_index],
        shaped[1, seq_index],
        shaped[2, seq_index],
        grad_shaped[seq_index],
        sums_list[seq_index],
        block_rows,
        score_scale,
    )
    grad_proj = jnp.stack(
        [
            grad_q_seq.reshape(group_rows, col_count),
            grad_k_seq.reshape(group_rows, col_count),
            grad_v_seq.reshape(group_rows, col_count),
        ]
    )
    grad_head = jnp.sum(grad_proj[0::2], axis=1, dtype=jnp.float32)[:, None, :]
    grad_input = jnp.einsum("td,itc->idc", norm_rows, grad_proj, preferred_element_type=jnp.float32)
    piece = grad_proj
    grad_first = lax.psum_scatter(
        jnp.einsum("itc,idc->td", piece, back_input, preferred_element_type=jnp.float32).astype(
            jnp.bfloat16
        ),
        "tensor",
        scatter_dimension=0,
        tiled=True,
    ).astype(jnp.float32)
    grad_tokens = grad_resid + norm_backward(grad_first, normed_one, inverse_one, gain_vals[0])
    gain_terms = jnp.stack(
        [jnp.sum(grad_first * normed_one, axis=0), jnp.sum(grad_second * normed_two, axis=0)]
    )
    offset_terms = jnp.stack(
        [
            jnp.sum(grad_first, axis=0),
            jnp.sum(grad_branch, axis=0, dtype=jnp.float32),
            jnp.sum(grad_second, axis=0),
            jnp.sum(cotangent, axis=0, dtype=jnp.float32),
        ]
    )
    gain_total, offset_total = packed_total((gain_terms, offset_terms), "tensor")
    (
        part_input,
        part_output,
        part_expand,
        part_contract,
        part_head,
        part_hidden_bias,
        part_gains,
        part_offsets,
    ) = (
        summed_rows_2(grad_input.astype(jnp.bfloat16), (("dp_0", "dp_1"), "dp_2"), 1),
        summed_rows_2(grad_output.astype(jnp.bfloat16), (("dp_0", "dp_1"), "dp_2"), 1),
        summed_rows_2(grad_expand.astype(jnp.bfloat16), (("dp_0", "dp_1"), "dp_2"), 0),
        summed_rows_2(grad_contract.astype(jnp.bfloat16), (("dp_0", "dp_1"), "dp_2"), 1),
        summed_rows_2(grad_head.astype(jnp.bfloat16), (("dp_0", "dp_1"), "dp_2"), 2),
        summed_rows_2(grad_hidden_bias.astype(jnp.bfloat16), (("dp_0", "dp_1"), "dp_2"), 1),
        *sent_together(
            (gain_total.astype(jnp.bfloat16), offset_total.astype(jnp.bfloat16)),
            (("dp_0", "dp_1"), "dp_2"),
            1,
            0,
        ),
    )
    return (
        output,
        grad_tokens,
        part_input,
        part_output,
        part_expand,
        part_contract,
        part_head,
        part_hidden_bias,
        part_gains,
        part_offsets,
    )


def solution(mesh):
    split = Mesh(
        mesh.devices.reshape(4, 2, 2, mesh.shape["tensor"]), ("dp_0", "dp_1", "dp_2", "tensor")
    )
    placed = (
        P(DP_TENSOR, None),
        P(None, DP, "tensor"),
        P("tensor", DP),
        P(DP, "tensor"),
        P("tensor", DP),
        P(None, "tensor", DP),
        P("tensor", DP),
        P(None, DP),
        P(None, DP),
        P(DP_TENSOR, None),
    )
    return jax.shard_map(
        per_device,
        mesh=split,
        in_specs=placed,
        out_specs=(
            P(DP_TENSOR, None),
            P(DP_TENSOR, None),
            P(None, DP, "tensor"),
            P("tensor", DP),
            P(DP, "tensor"),
            P("tensor", DP),
            P(None, "tensor", DP),
            P("tensor", DP),
            P(None, DP),
            P(None, DP),
        ),
        check_vma=False,
    )
```

profile of v0, /device:TPU:0, one launch (start us, length us, event | category | flops | bytes accessed | tf_op | source)
XLA Modules:
  0.0 665.3 jit_solution(14223151543383056517)
XLA Ops:
  8.7 19.8 %all-gather = bf16[16,64,6]{1,2,0:T(8,128)(2,1)S(1)} all-gather(bf16[1,64,6]{1,2,0:T(8,128)(2,1)S(1)} %maximum_bitcast_fusion.3), channel_id=1, replica_groups=mesh['dp_0'=4,'dp_1'=2,'dp_2'=2,'tensor'=8] {'dp_0','dp_1','dp_2'}, dimensions={0}, use_global_device_ids=true | all-gather | bytes 13056 | tf_op jit(solution)/shard_map/all_gather | solution.py:22
  34.4 7.8 %all-to-all-start = ((bf16[8,128,1024]{2,1,0:T(8,128)(2,1)}), bf16[8,128,1024]{2,1,0:T(8,128)(2,1)S(1)}, u32[]{:S(2)}, u32[]{:S(2)}) async-start(bf16[8,128,1024]{2,1,0:T(8,128)(2,1)} %broadcast_in_dim.42), calls=%async_computation | async-start | bytes 4194304 | tf_op jit(solution)/shard_map/all_to_all | solution.py:28
  42.4 35.4 %all_gather.23 = bf16[2,1,128]{1,0,2:T(2,128)(2,1)S(1)} all-gather(bf16[2,1,8]{1,0,2:T(2,128)(2,1)S(1)} %copy.173), channel_id=1, replica_groups=mesh['dp_0'=4,'dp_1'=2,'dp_2'=2,'tensor'=8] {'dp_0','dp_1','dp_2'}, dimensions={2}, use_global_device_ids=true | all-gather | bytes 544 | tf_op jit(solution)/shard_map/all_gather | solution.py:205
  78.6 17.0 %all_gather.24 = bf16[128,1024]{0,1:T(8,128)(2,1)S(1)} all-gather(bf16[128,64]{0,1:T(8,128)(2,1)S(1)} %copy-done.35), channel_id=1, replica_groups=mesh['dp_0'=4,'dp_1'=2,'dp_2'=2,'tensor'=8] {'dp_0','dp_1','dp_2'}, dimensions={1}, use_global_device_ids=true | all-gather | bytes 278528 | tf_op jit(solution)/shard_map/all_gather | solution.py:202
  97.8 21.3 %all_gather.22 = bf16[3,1024,128]{2,1,0:T(8,128)(2,1)} all-gather(bf16[3,64,128]{2,1,0:T(8,128)(2,1)S(1)} %copy-done.30), channel_id=1, replica_groups=mesh['dp_0'=4,'dp_1'=2,'dp_2'=2,'tensor'=8] {'dp_0','dp_1','dp_2'}, dimensions={1}, use_global_device_ids=true | all-gather | bytes 835584 | tf_op jit(solution)/shard_map/all_gather | solution.py:201
  132.1 83.4 %reduce-scatter.5.cloned.1.call-done = f32[128,1024]{1,0:T(8,128)} async-done(((f32[1024,1024]{1,0:T(8,128)}), f32[128,1024]{1,0:T(8,128)}) %reduce-scatter.5.cloned.1.call-update) | async-done | bytes 524304 | tf_op jit(solution)/shard_map/reduce_scatter | solution.py:236
  219.9 4.4 all-to-all-start.1
  224.9 28.2 %all-to-all-done.1 = bf16[8,128,1024]{2,1,0:T(8,128)(2,1)} async-done(((bf16[8,128,1024]{2,1,0:T(8,128)(2,1)}), bf16[8,128,1024]{2,1,0:T(8,128)(2,1)}, u32[]{:S(2)}, u32[]{:S(2)}) %all-to-all-start.1) | async-done | bytes 2097184 | tf_op jit(solution)/shard_map/all_to_all | solution.py:28
  255.6 4.4 all-to-all-start.2
  263.8 38.6 %all-reduce.2 = bf16[512]{0:T(512)(128)(2,1)} all-reduce(bf16[512]{0:T(512)(128)(2,1)} %dynamic-update-slice.10), channel_id=1, replica_groups=mesh['dp_0'=4,'dp_1'=2,'dp_2'=2,'tensor'=8] {'dp_0','dp_1','dp_2'}, use_global_device_ids=true, to_apply=%add.2 | all-reduce | flops 512 | bytes 2048
  303.7 4.4 fusion.68
  308.2 6.0 fusion.58
  317.9 4.7 convolution_convert_fusion.1
  322.6 69.6 %reduce-scatter.9.cloned.1.call-done = bf16[128,1024]{1,0:T(8,128)(2,1)} async-done(((bf16[1024,1024]{1,0:T(8,128)(2,1)}), bf16[128,1024]{1,0:T(8,128)(2,1)}) %reduce-scatter.9.cloned.1.call-update) | async-done | bytes 262160 | tf_op jit(solution)/shard_map/reduce_scatter | solution.py:280
  394.5 75.7 %reduce-scatter.7.cloned.1.call-done = bf16[128,1024]{1,0:T(8,128)(2,1)} async-done(((bf16[1024,1024]{1,0:T(8,128)(2,1)}), bf16[128,1024]{1,0:T(8,128)(2,1)}) %reduce-scatter.7.cloned.1.call-update) | async-done | bytes 262160 | tf_op jit(solution)/shard_map/reduce_scatter | solution.py:255
  474.8 4.5 all-to-all-start.3
  479.6 25.0 %all-to-all-done.3 = bf16[8,128,1024]{2,1,0:T(8,128)(2,1)} async-done(((bf16[8,128,1024]{2,1,0:T(8,128)(2,1)}), bf16[8,128,1024]{2,1,0:T(8,128)(2,1)}, u32[]{:S(2)}, u32[]{:S(2)}) %all-to-all-start.3) | async-done | bytes 2097184 | tf_op jit(solution)/shard_map/all_to_all | solution.py:28
  515.3 4.3 multiply_convert_fusion
  537.5 4.6 all_to_all.97
  542.0 4.6 all_to_all.98
  546.6 4.2 all-to-all-start.15
  552.0 4.9 all-to-all-done.15
  562.0 7.9 %all-to-all-done.11 = bf16[8,512,64]{1,2,0:T(8,128)(2,1)S(1)} async-done(((bf16[8,512,64]{1,2,0:T(8,128)(2,1)}), bf16[8,512,64]{1,2,0:T(8,128)(2,1)S(1)}, u32[]{:S(2)}, u32[]{:S(2)}) %all-to-all-start.11) | async-done | bytes 524320 | tf_op jit(solution)/shard_map/all_to_all | solution.py:72
  573.5 4.4 all-to-all-start.9
  587.8 3.9 all_to_all.100
  591.7 4.4 all_to_all.101
  600.6 4.8 all-to-all-done.13
  610.6 4.6 all-to-all-done.7
  621.6 4.4 all-to-all-done.5
  629.0 5.2 all-to-all-start.16
  634.1 8.4 %all-to-all-done.16 = f32[8,1,6144]{2,1,0:T(1,128)S(1)} async-done(((f32[8,1,6144]{2,1,0:T(1,128)}), f32[8,1,6144]{2,1,0:T(1,128)S(1)}, u32[]{:S(2)}, u32[]{:S(2)}) %all-to-all-start.16) | async-done | bytes 196640 | tf_op jit(solution)/shard_map/all_to_all | solution.py:28
  651.9 5.0 all-to-all-done.18
  (259 shorter events, 122.8 us)
Async XLA Ops:
  34.4 44.2 %copy-start.35 = (bf16[128,64]{0,1:T(8,128)(2,1)S(1)}, bf16[128,64]{0,1:T(8,128)(2,1)}, u32[]{:S(2)}) copy-start(bf16[128,64]{0,1:T(8,128)(2,1)} %param.24) | copy-start | bytes 49156
  34.4 63.4 %copy-start.30 = (bf16[3,64,128]{2,1,0:T(8,128)(2,1)S(1)}, bf16[3,64,128]{2,1,0:T(8,128)(2,1)}, u32[]{:S(2)}) copy-start(bf16[3,64,128]{2,1,0:T(8,128)(2,1)} %param.23) | copy-start | bytes 147460
  34.4 84.6 %all-to-all-start = ((bf16[8,128,1024]{2,1,0:T(8,128)(2,1)}), bf16[8,128,1024]{2,1,0:T(8,128)(2,1)S(1)}, u32[]{:S(2)}, u32[]{:S(2)}) async-start(bf16[8,128,1024]{2,1,0:T(8,128)(2,1)} %broadcast_in_dim.42), calls=%async_computation | async-start | bytes 4194304 | tf_op jit(solution)/shard_map/all_to_all | solution.py:28
  42.2 173.4 %reduce-scatter.5.cloned.1.call-start = ((), (), s32[]{:S(2)}) async-start(), calls=%async_computation.23 | async-start | bytes 4718592 | tf_op jit(solution)/shard_map/reduce_scatter | solution.py:236
  131.5 84.1 %copy-start.2 = (bf16[128,1024]{1,0:T(8,128)(2,1)S(1)}, bf16[128,1024]{1,0:T(8,128)(2,1)}, u32[]{:S(2)}) copy-start(bf16[128,1024]{1,0:T(8,128)(2,1)} %param.22) | copy-start | bytes 786436
  131.5 172.2 %all-gather.4.cloned.1.call-start = ((), (), s32[]{:S(2)}) async-start(), calls=%async_computation.24 | async-start | bytes 1114112 | tf_op jit(solution)/shard_map/all_gather | solution.py:203
  219.9 33.1 %all-to-all-start.1 = ((bf16[8,128,1024]{2,1,0:T(8,128)(2,1)}), bf16[8,128,1024]{2,1,0:T(8,128)(2,1)}, u32[]{:S(2)}, u32[]{:S(2)}) async-start(bf16[8,128,1024]{2,1,0:T(8,128)(2,1)} %broadcast_in_dim.47), calls=%async_computation.2 | async-start | bytes 4194304 | tf_op jit(solution)/shard_map/all_to_all | solution.py:28
  224.3 83.9 %all-gather.6.cloned.1.call-start = ((), (), s32[]{:S(2)}) async-start(), calls=%async_computation.25 | async-start | bytes 1114112 | tf_op jit(solution)/shard_map/all_gather | solution.py:204
  255.6 52.6 %all-to-all-start.2 = ((bf16[8,128,1024]{2,1,0:T(8,128)(2,1)}), bf16[8,128,1024]{2,1,0:T(8,128)(2,1)}, u32[]{:S(2)}, u32[]{:S(2)}) async-start(bf16[8,128,1024]{2,1,0:T(8,128)(2,1)} %broadcast_in_dim.48), calls=%async_computation.4 | async-start | bytes 4194304 | tf_op jit(solution)/shard_map/all_to_all | solution.py:28
  260.0 132.2 %reduce-scatter.9.cloned.1.call-start = ((), (), s32[]{:S(2)}) async-start(), calls=%async_computation.27 | async-start | bytes 2359296 | tf_op jit(solution)/shard_map/reduce_scatter | solution.py:280
  317.8 152.4 %reduce-scatter.7.cloned.1.call-start = ((), (), s32[]{:S(2)}) async-start(), calls=%async_computation.26 | async-start | bytes 2359296 | tf_op jit(solution)/shard_map/reduce_scatter | solution.py:255
  474.8 29.8 %all-to-all-start.3 = ((bf16[8,128,1024]{2,1,0:T(8,128)(2,1)}), bf16[8,128,1024]{2,1,0:T(8,128)(2,1)}, u32[]{:S(2)}, u32[]{:S(2)}) async-start(bf16[8,128,1024]{2,1,0:T(8,128)(2,1)} %broadcast_in_dim.49), calls=%async_computation.6 | async-start | bytes 4194304 | tf_op jit(solution)/shard_map/all_to_all | solution.py:28
  479.3 147.4 %reduce-scatter.11.cloned.1.call-start = ((), (), s32[]{:S(2)}) async-start(), calls=%async_computation.28 | async-start | bytes 2359296 | tf_op jit(solution)/shard_map/reduce_scatter | solution.py:318
  546.6 10.3 %all-to-all-start.15 = ((bf16[8,1,32]{2,1,0:T(2,128)(2,1)}), bf16[8,1,32]{2,1,0:T(2,128)(2,1)S(1)}, u32[]{:S(2)}, u32[]{:S(2)}) async-start(bf16[8,1,32]{2,1,0:T(2,128)(2,1)} %copy.195), calls=%async_computation.19 | async-start | bytes 8192 | tf_op jit(solution)/shard_map/all_to_all | solution.py:72
  550.8 10.7 %copy-start.10 = (bf16[1,1024,128]{2,1,0:T(8,128)(2,1)S(1)}, bf16[1,1024,128]{2,1,0:T(8,128)(2,1)}, u32[]{:S(2)}) copy-start(bf16[1,1024,128]{2,1,0:T(8,128)(2,1)} %copy-done.9) | copy-start | bytes 786436
  550.8 10.7 %copy-start.12 = (bf16[1,1024,128]{2,1,0:T(8,128)(2,1)S(1)}, bf16[1,1024,128]{2,1,0:T(8,128)(2,1)}, u32[]{:S(2)}) copy-start(bf16[1,1024,128]{2,1,0:T(8,128)(2,1)} %copy-done.11) | copy-start | bytes 786436
  556.9 12.9 %all-to-all-start.11 = ((bf16[8,512,64]{1,2,0:T(8,128)(2,1)}), bf16[8,512,64]{1,2,0:T(8,128)(2,1)S(1)}, u32[]{:S(2)}, u32[]{:S(2)}) async-start(bf16[8,512,64]{1,2,0:T(8,128)(2,1)} %reduce_sum.368), calls=%async_computation.15 | async-start | bytes 1048576 | tf_op jit(solution)/shard_map/all_to_all | solution.py:72
  560.4 17.5 %copy-start.15 = (bf16[2,64,512]{2,1,0:T(8,128)(2,1)S(1)}, bf16[2,64,512]{2,1,0:T(8,128)(2,1)}, u32[]{:S(2)}) copy-start(bf16[2,64,512]{2,1,0:T(8,128)(2,1)} %copy-done.14) | copy-start | bytes 393220
  573.5 14.2 %all-to-all-start.9 = ((bf16[8,64,512]{2,1,0:T(8,128)(2,1)}), bf16[8,64,512]{2,1,0:T(8,128)(2,1)}, u32[]{:S(2)}, u32[]{:S(2)}) async-start(bf16[8,64,512]{2,1,0:T(8,128)(2,1)} %reduce_sum.366), calls=%async_computation.13 | async-start | bytes 1048576 | tf_op jit(solution)/shard_map/all_to_all | solution.py:72
  596.0 9.4 %all-to-all-start.13 = ((bf16[8,2,1,8]{3,1,2,0:T(2,128)(2,1)}), bf16[8,2,1,8]{3,1,2,0:T(2,128)(2,1)S(1)}, u32[]{:S(2)}, u32[]{:S(2)}) async-start(bf16[8,2,1,8]{3,1,2,0:T(2,128)(2,1)} %copy.193), calls=%async_computation.17 | async-start | bytes 8192 | tf_op jit(solution)/shard_map/all_to_all | solution.py:72
  600.6 26.1 %copy-start.41 = (f32[128]{0:T(128)S(1)}, f32[128]{0:T(128)}, u32[]{:S(2)}) copy-start(f32[128]{0:T(128)} %copy-done.40) | copy-start | bytes 1540
  600.6 26.1 %copy-start.44 = (f32[128]{0:T(128)S(1)}, f32[128]{0:T(128)}, u32[]{:S(2)}) copy-start(f32[128]{0:T(128)} %copy-done.43) | copy-start | bytes 1540
  605.4 9.7 %all-to-all-start.7 = ((bf16[8,128,64]{1,2,0:T(8,128)(2,1)}), bf16[8,128,64]{1,2,0:T(8,128)(2,1)S(1)}, u32[]{:S(2)}, u32[]{:S(2)}) async-start(bf16[8,128,64]{1,2,0:T(8,128)(2,1)} %reduce_sum.364), calls=%async_computation.11 | async-start | bytes 262144 | tf_op jit(solution)/shard_map/all_to_all | solution.py:72
  608.8 19.2 %copy-start.31 = (f32[1024]{0:T(1024)S(1)}, f32[1024]{0:T(1024)}, u32[]{:S(2)}) copy-start(f32[1024]{0:T(1024)} %get-tuple-element.154) | copy-start | bytes 12292
  609.6 18.5 %copy-start.32 = (f32[1024]{0:T(1024)S(1)}, f32[1024]{0:T(1024)}, u32[]{:S(2)}) copy-start(f32[1024]{0:T(1024)} %get-tuple-element.161) | copy-start | bytes 12292
  609.6 18.5 %copy-start.33 = (f32[1024]{0:T(1024)S(1)}, f32[1024]{0:T(1024)}, u32[]{:S(2)}) copy-start(f32[1024]{0:T(1024)} %get-tuple-element.164) | copy-start | bytes 12292
  609.6 18.6 %copy-start.34 = (f32[1024]{0:T(1024)S(1)}, f32[1024]{0:T(1024)}, u32[]{:S(2)}) copy-start(f32[1024]{0:T(1024)} %get-tuple-element.178) | copy-start | bytes 12292
  610.6 40.3 %copy-start.5 = (f32[128,1024]{1,0:T(8,128)S(1)}, f32[128,1024]{1,0:T(8,128)}, u32[]{:S(2)}) copy-start(f32[128,1024]{1,0:T(8,128)} %get-tuple-element.166) | copy-start | bytes 1572868
  615.2 10.9 %all-to-all-start.5 = ((bf16[8,3,64,128]{3,2,1,0:T(8,128)(2,1)}), bf16[8,3,64,128]{3,2,1,0:T(8,128)(2,1)S(1)}, u32[]{:S(2)}, u32[]{:S(2)}) async-start(bf16[8,3,64,128]{3,2,1,0:T(8,128)(2,1)} %reduce_sum.362), calls=%async_computation.9 | async-start | bytes 786432 | tf_op jit(solution)/shard_map/all_to_all | solution.py:72
  626.7 24.1 %copy-start.8 = (bf16[128,1024]{1,0:T(8,128)(2,1)S(1)}, bf16[128,1024]{1,0:T(8,128)(2,1)}, u32[]{:S(2)}) copy-start(bf16[128,1024]{1,0:T(8,128)(2,1)} %reduce-scatter.11.cloned.1.call-done) | copy-start | bytes 786436
  629.0 13.6 %all-to-all-start.16 = ((f32[8,1,6144]{2,1,0:T(1,128)}), f32[8,1,6144]{2,1,0:T(1,128)S(1)}, u32[]{:S(2)}, u32[]{:S(2)}) async-start(f32[8,1,6144]{2,1,0:T(1,128)} %broadcast_in_dim.50), calls=%async_computation.20 | async-start | bytes 393216 | tf_op jit(solution)/shard_map/all_to_all | solution.py:28
  647.5 9.4 %all-to-all-start.18 = ((bf16[8,2,192]{2,1,0:T(2,128)(2,1)}), bf16[8,2,192]{2,1,0:T(2,128)(2,1)S(1)}, u32[]{:S(2)}, u32[]{:S(2)}) async-start(bf16[8,2,192]{2,1,0:T(2,128)(2,1)} %reshape.434), calls=%async_computation.22 | async-start | bytes 16384 | tf_op jit(solution)/shard_map/all_to_all | solution.py:72
  (39 other events, 117.3 us)
Sparse Core Ops, SparseCore 0:
  131.7 83.8 reduce-scatter.4
  318.0 74.1 reduce-scatter.8
  396.4 73.8 reduce-scatter.6
  524.4 79.4 reduce-scatter.10
Sparse Core Ops, SparseCore 1:
  133.8 36.4 all-gather.3
  226.6 34.5 all-gather.5
where the time goes:
time: 667 us; the launch traced here: 665 us
  waiting for transfers between devices  325 us (49%)
  blocking collectives  161 us (24%)
  starting transfers between devices  52.3 us (8%)
  matrix products  48.7 us (7%)
  other arithmetic  33 us (5%)
  local copies, waits for them, and re-layouts  28.7 us (4%)
  between operations  16.8 us (3%)
    reduce_scatter x1, waiting for transfers between devices, per_device(): lax.psum_scatter(jnp.dot(piece, full_output, preferred_element_type=jnp.f...  83.4 us
    reduce_scatter x1, waiting for transfers between devices, per_device(): lax.psum_scatter(jnp.dot(piece, full_contract, preferred_element_type=jnp...  75.7 us
    reduce_scatter x1, waiting for transfers between devices, per_device(): lax.psum_scatter(jnp.einsum('th,dh->td', piece, back_expand, preferred_el...  69.6 us
    all_to_all x5, waiting for transfers between devices, sent_to_all(): lax.all_to_all(jnp.broadcast_to(value[None], (devices, *value.shape)), ax...  61.6 us
    unnamed x1, blocking collectives  38.6 us
    all_gather x1, blocking collectives, per_device(): lax.all_gather(head_bias, DP, axis=2, tiled=True)  35.4 us
    all_to_all x7, waiting for transfers between devices, summed_rows_2(): lax.all_to_all(own.astype(jnp.bfloat16), far, 0, 0, tiled=True)  33.9 us
    all_to_all x7, blocking collectives, sent_and_summed(): lax.all_to_all(in_blocks(value, dim, devices), axis, 0, 0, tiled=True)  28.5 us
  transfers between devices with their start and end apart: 18, of which 13 were waited for; matrix products, arithmetic and copies ran while one was open for 8% of the time, Pallas kernels for 0%

commit v1 on v0

v1 whole, which is shorter than its diff:
```python
import functools

import jax
import jax.numpy as jnp
from jax import lax
from jax.experimental import pallas as pl
from jax.experimental.pallas import tpu as pltpu
from jax.sharding import Mesh
from jax.sharding import PartitionSpec as P

F32, BF16 = jnp.float32, jnp.bfloat16
MESH = pl.DeviceIdType.MESH
DP = ("x", "yl", "c")
TENSOR = ("yh", "z")
EPSILON = 1e-05
MASKED = -1000000000.0
GELU_COEF = 0.7978845608028654
CUBIC = 0.044715
SCALE = 64 ** (-0.5)
N_SEMS = 340


def nn(a, b):
    return lax.dot_general(a, b, (((1,), (0,)), ((), ())), preferred_element_type=F32)


def nt(a, b):
    return lax.dot_general(a, b, (((1,), (1,)), ((), ())), preferred_element_type=F32)


def tn(a, b):
    return lax.dot_general(a, b, (((0,), (0,)), ((), ())), preferred_element_type=F32)


def rows(start, size, by=None):
    if isinstance(start, int):
        return pl.ds(start, size)
    return pl.ds(pl.multiple_of(start, by or size), size)


def norm_rows(v):
    shifted = v - jnp.mean(v, axis=-1, keepdims=True)
    inverse = lax.rsqrt(jnp.mean(shifted * shifted, axis=-1, keepdims=True) + EPSILON)
    return shifted * inverse, inverse


def norm_back(grad, normed, inverse, gain):
    scaled = grad * gain
    first = jnp.mean(scaled, axis=-1, keepdims=True)
    second = jnp.mean(scaled * normed, axis=-1, keepdims=True)
    return inverse * (scaled - first - normed * second)


class Links:
    def __init__(self, send_sems, recv_sems):
        self.send_sems, self.recv_sems = send_sems, recv_sems
        self.sent, self.received, self.open = 0, 0, []

    def slots(self, count):
        first = self.received
        self.received += count
        assert self.received <= N_SEMS
        return first

    def make(self, src, dst, recv, to):
        copy = pltpu.make_async_remote_copy(
            src_ref=src,
            dst_ref=dst,
            send_sem=self.send_sems.at[self.sent],
            recv_sem=self.recv_sems.at[recv],
            device_id=to,
            device_id_type=MESH,
        )
        self.sent += 1
        assert self.sent <= N_SEMS
        return copy

    def send(self, src, dst, recv, to):
        copy = self.make(src, dst, recv, to)
        copy.start()
        self.open.append((None, copy))

    def send_if(self, cond, src, dst, recv, to):
        copy = self.make(src, dst, recv, to)
        pl.when(cond)(copy.start)
        self.open.append((cond, copy))

    def local_if(self, cond, src, dst, recv):
        copy = pltpu.make_async_copy(src, dst, self.recv_sems.at[recv])
        pl.when(cond)(copy.start)

    def wait(self, recv, ref, to):
        pltpu.make_async_remote_copy(
            src_ref=ref,
            dst_ref=ref,
            send_sem=self.send_sems.at[0],
            recv_sem=self.recv_sems.at[recv],
            device_id=to,
            device_id_type=MESH,
        ).wait_recv()

    def drain(self):
        for cond, copy in self.open:
            if cond is None:
                copy.wait_send()
            else:
                pl.when(cond)(copy.wait_send)
        self.open = []


class Ring:
    def __init__(self, links, axis, pos):
        self.links, self.axis = links, axis
        self.pos = pos
        self.right, self.left, self.far = (lax.rem(pos + k, 4) for k in (1, 3, 2))
        self.to_right, self.to_left = {axis: self.right}, {axis: self.left}


class RingGather:
    def __init__(self, ring, buf, offset, half, partner=None, offset_partner=None):
        self.ring, self.buf, self.offset, self.half = ring, buf, offset, half
        self.partner, self.offset_partner = partner, offset_partner
        self.ids = ring.links.slots(6)
        if partner is not None:
            self.pids = ring.links.slots(8)

    def at(self, pos, part, offset=None):
        return self.buf.at[rows((offset or self.offset)(pos) + part * self.half, self.half)]

    def relay(self, pos, part, slot):
        if self.partner is not None:
            ref = self.at(pos, part)
            self.ring.links.send(ref, ref, self.pids + slot, self.partner)

    def start(self):
        r, s = self.ring, self.ring.links.send
        a, b = self.at(r.pos, 0), self.at(r.pos, 1)
        s(a, a, self.ids + 0, r.to_right)
        s(b, b, self.ids + 3, r.to_left)
        s(b, b, self.ids + 1, r.to_right)
        s(a, a, self.ids + 2, r.to_left)
        self.relay(r.pos, 0, 0)
        self.relay(r.pos, 1, 1)

    def forward(self):
        r, s, w = self.ring, self.ring.links.send, self.ring.links.wait
        ref = self.at(r.left, 0)
        w(self.ids + 0, ref, r.to_left)
        s(ref, ref, self.ids + 4, r.to_right)
        ref = self.at(r.right, 1)
        w(self.ids + 3, ref, r.to_right)
        s(ref, ref, self.ids + 5, r.to_left)
        self.relay(r.left, 0, 2)
        self.relay(r.right, 1, 5)

    def done(self):
        r, w = self.ring, self.ring.links.wait
        w(self.ids + 1, self.at(r.left, 1), r.to_left)
        self.relay(r.left, 1, 3)
        w(self.ids + 2, self.at(r.right, 0), r.to_right)
        self.relay(r.right, 0, 4)
        w(self.ids + 4, self.at(r.far, 0), r.to_left)
        self.relay(r.far, 0, 6)
        w(self.ids + 5, self.at(r.far, 1), r.to_right)
        self.relay(r.far, 1, 7)
        if self.partner is not None:
            order = ((r.pos, 0), (r.pos, 1), (r.left, 0), (r.left, 1))
            order += ((r.right, 0), (r.right, 1), (r.far, 0), (r.far, 1))
            for slot, (pos, part) in enumerate(order):
                w(self.pids + slot, self.at(pos, part, self.offset_partner), self.partner)


class RingSum:
    def __init__(self, ring, buf, offset, half, land):
        self.ring, self.buf, self.offset, self.half, self.land = ring, buf, offset, half, land
        self.ids = ring.links.slots(6)

    def at(self, pos, part, count=1):
        return self.buf.at[rows(self.offset(pos) + part * self.half, self.half * count, self.half)]

    def landing(self, slot):
        return self.land.at[pl.ds(slot * self.half, self.half)]

    def send(self, src, slot, to):
        self.ring.links.send(src, self.landing(slot), self.ids + slot, to)

    def wait(self, slot, to):
        self.ring.links.wait(self.ids + slot, self.landing(slot), to)

    def add(self, pos, part, slot):
        ref = self.at(pos, part)
        ref[...] = (ref[...].astype(F32) + self.landing(slot)[...].astype(F32)).astype(BF16)

    def send_far(self):
        r = self.ring
        self.send(self.at(r.far, 0), 0, r.to_right)
        self.send(self.at(r.far, 1), 1, r.to_left)

    def send_near(self):
        r = self.ring
        self.send(self.at(r.right, 1), 3, r.to_right)
        self.send(self.at(r.left, 0), 4, r.to_left)

    def middle(self):
        r = self.ring
        self.wait(0, r.to_left)
        self.add(r.right, 0, 0)
        self.send(self.at(r.right, 0), 2, r.to_right)
        self.wait(1, r.to_right)
        self.add(r.left, 1, 1)
        self.send(self.at(r.left, 1), 5, r.to_left)

    def total(self):
        r = self.ring
        self.wait(3, r.to_left)
        self.wait(4, r.to_right)
        self.wait(2, r.to_left)
        self.wait(5, r.to_right)
        own = self.at(r.pos, 0, 2)[...].astype(F32)
        left = self.land[pl.ds(2 * self.half, 2 * self.half)].astype(F32)
        right = self.land[pl.ds(4 * self.half, 2 * self.half)].astype(F32)
        return own + left + right


class GroupSum:
    def __init__(self, ring, c, buf, from_core, land):
        self.links, self.c, self.buf, self.from_core = ring.links, c, buf, from_core
        self.partner = {"c": 1 - c}
        self.order = (ring.far, ring.right, ring.left, ring.pos)
        self.ids = ring.links.slots(4)
        self.sum = RingSum(ring, buf, lambda p: c * 512 + p * 128, 64, land)

    def core_send(self):
        for k, pos in enumerate(self.order):
            src = self.buf.at[rows((1 - self.c) * 512 + pos * 128, 128)]
            dst = self.from_core.at[rows(pos * 128, 128)]
            self.links.send(src, dst, self.ids + k, self.partner)

    def core_add(self, k):
        got = self.from_core.at[rows(self.order[k] * 128, 128)]
        self.links.wait(self.ids + k, got, self.partner)
        ref = self.buf.at[rows(self.c * 512 + self.order[k] * 128, 128)]
        ref[...] = (ref[...].astype(F32) + got[...].astype(F32)).astype(BF16)

    def start(self):
        self.core_add(0)
        self.sum.send_far()
        self.core_add(1)
        self.core_add(2)
        self.sum.send_near()

    def middle(self):
        self.sum.middle()
        self.core_add(3)

    def total(self):
        return self.sum.total()


class WeightGather:
    def __init__(self, ring, me, buf, size, shard):
        self.ring, self.me, self.buf, self.size, self.shard = ring, me, buf, size, shard
        self.ids = ring.links.slots(4)
        self.gather = RingGather(ring, buf, lambda p: p * 4 * size, 2 * size)

    def start(self):
        x, yl, c, yh, z = self.me
        links = self.ring.links
        own = self.buf.at[rows((x * 4 + yl * 2 + c) * self.size, self.size)]
        slot = self.ids + yl * 2 + c
        for dl, dh in ((1, 0), (0, 1), (1, 1)):
            to = {"yl": lax.rem(yl + dl, 2), "yh": lax.rem(yh + dh, 2), "c": yh}
            links.send(self.shard, own, slot, to)
        links.local_if(c == yh, self.shard, own, slot)
        links.send_if(c != yh, self.shard, own, slot, {"c": yh})

    def start_x(self):
        x, yl, c, yh, z = self.me
        for k in range(4):
            ref = self.buf.at[rows((x * 4 + k) * self.size, self.size)]
            self.ring.links.wait(self.ids + k, ref, {"c": 1 - c})
        self.gather.start()


class WeightSum:
    def __init__(self, ring, me, buf, size, land, land_y):
        self.ring, self.me, self.buf, self.size = ring, me, buf, size
        self.land_y = land_y
        self.sum = RingSum(ring, buf, lambda p: p * 4 * size, 2 * size, land)
        self.ids = ring.links.slots(4)

    def start(self):
        self.sum.send_far()
        self.sum.send_near()

    def middle(self):
        self.sum.middle()

    def start_y(self):
        x, yl, c, yh, z = self.me
        links, size = self.ring.links, self.size
        total = self.sum.total()
        self.buf[rows(x * 4 * size, 4 * size)] = total.astype(BF16)
        slot = yh * 2 + yl
        dst = self.land_y.at[rows(slot * size, size)]
        for dl, dc in ((1, 0), (0, 1), (1, 1), (0, 0)):
            to_l, to_c = lax.rem(yl + dl, 2), lax.rem(c + dc, 2)
            src = self.buf.at[rows((x * 4 + to_l * 2 + to_c) * size, size)]
            if dl or dc:
                links.send(src, dst, self.ids + slot, {"yl": to_l, "c": to_c, "yh": c})
            else:
                links.local_if(c == yh, src, dst, self.ids + slot)
                links.send_if(c != yh, src, dst, self.ids + slot, {"yh": c})

    def finish(self):
        c = self.me[2]
        total = 0.0
        for k in range(4):
            ref = self.land_y.at[pl.ds(k * self.size, self.size)]
            self.ring.links.wait(self.ids + k, ref, {"c": 1 - c})
            total = total + ref[...].astype(F32)
        return total


def layer_kernel(
    tok_ref, cot_ref, wi_ref, wo_ref, we_ref, wc_ref, sm_ref,
    out_ref, gtok_ref, gwi_ref, gwo_ref, gwe_ref, gwc_ref, gsm_ref,
    xg, cotg, h1, h2, gbg, wi, wo, we, wc, sm, gi, go, ge, gc, gs,
    land_i, land_o, land_e, land_c, land_s, landy_i, landy_o, landy_e, landy_c, landy_s,
    part_b, part_o, part_2, part_1, core_b, core_o, core_2, core_1, near_b, near_o, near_2, near_1,
    qkv, gqkv, kvr, gkv_out, gkv_in, att, gatt, hid, gp, lse, dk_acc, dv_acc, dk0_acc, dv0_acc,
    resid, gres, vec, tens, hb_sum, send_sems, recv_sems,
):
    x, yl, c, yh, z = me = tuple(lax.axis_index(a) for a in ("x", "yl", "c", "yh", "z"))
    links = Links(send_sems, recv_sems)
    ring_z, ring_x = Ring(links, "z", z), Ring(links, "x", x)
    partner = {"c": 1 - c}

    def block(p):
        return c * 512 + p * 128

    def block_partner(p):
        return (1 - c) * 512 + p * 128

    barrier = pltpu.get_barrier_semaphore()
    peers = [{"x": ring_x.right}, {"x": ring_x.left}]
    for dh in range(2):
        for dz in range(4):
            if dh or dz:
                peers.append({"yh": lax.rem(yh + dh, 2), "z": lax.rem(z + dz, 4)})
    for dl in range(2):
        for dc in range(2):
            for dh in range(2):
                if dl or dc:
                    peers.append({"yl": lax.rem(yl + dl, 2), "c": lax.rem(c + dc, 2), "yh": lax.rem(yh + dh, 2)})
    for peer in peers:
        pl.semaphore_signal(barrier, inc=1, device_id=peer, device_id_type=MESH)
    own = rows(block(z), 128)
    xg[own] = tok_ref[...]
    cotg[own] = cot_ref[...]
    pl.semaphore_wait(barrier, len(peers))

    gather_x = RingGather(ring_z, xg, block, 64, partner, block_partner)
    gather_x.start()
    w_sm = WeightGather(ring_x, me, sm, 16, sm_ref)
    w_i = WeightGather(ring_x, me, wi, 64, wi_ref)
    w_o = WeightGather(ring_x, me, wo, 64, wo_ref)
    w_e = WeightGather(ring_x, me, we, 64, we_ref)
    w_c = WeightGather(ring_x, me, wc, 64, wc_ref)
    for w in (w_sm, w_i, w_o, w_e, w_c):
        w.start()
    w_sm.start_x()
    w_i.start_x()
    gather_x.forward()
    w_sm.gather.forward()
    w_i.gather.forward()
    gather_x.done()
    gather_c = RingGather(ring_z, cotg, block, 64, partner, block_partner)
    gather_c.start()
    w_sm.gather.done()

    tiles = [sm[pl.ds(16 * k, 16)].astype(F32) for k in range(16)]
    pairs = [tiles[2 * k] + tiles[2 * k + 1] for k in range(8)]
    vectors = jnp.concatenate(pairs, axis=1)
    gains, offs = vectors[0:2], vectors[2:6]
    fours = [pairs[2 * k] + pairs[2 * k + 1] for k in range(4)]
    hidden_bias = jnp.concatenate([f[6:7] for f in fours], axis=1)
    every = fours[0] + fours[1] + fours[2] + fours[3]
    qkv_bias = jnp.concatenate([every[7:8], jnp.zeros((1, 128), F32), every[8:9]], axis=1)
    gain1, gain2 = gains[0:1], gains[1:2]
    off0, off1, off2, off3 = (offs[k : k + 1] for k in range(4))

    w_i.gather.done()

    @pl.loop(0, 4)
    def _(i):
        r = rows(i * 256, 256)
        normed, _ = norm_rows(xg[r].astype(F32))
        low = (normed * gain1 + off0).astype(BF16)
        h1[r] = low
        qkv[r] = (nn(low, wi[...]) + qkv_bias).astype(BF16)

    kv_slot = links.slots(1)
    links.send_if(yh == 0, qkv.at[:, pl.ds(128, 256)], kvr, kv_slot, {"yh": 1})
    w_o.start_x()
    w_e.start_x()
    w_c.start_x()
    gather_c.forward()

    lane = lax.broadcasted_iota(jnp.int32, (1, 128), 1)
    head_lanes = [lane < 64, lane >= 64]

    def causal(scores, first):
        r = lax.broadcasted_iota(jnp.int32, scores.shape, 0) + first
        return jnp.where(r >= lax.broadcasted_iota(jnp.int32, scores.shape, 1), scores, MASKED)

    def masked(value, h):
        return jnp.where(head_lanes[h], value, jnp.zeros_like(value))

    def attend(remote):
        @pl.loop(0, 2)
        def _(s):
            for qb in range(2):
                nk = 256 * (qb + 1)
                r = rows(s * 512 + qb * 256, 256)
                keys = rows(s * 512, nk, 512)
                q, k, v = qkv[r, 0:128], qkv[keys, 128:256], qkv[keys, 256:384]
                outs = []
                for h in range(2):
                    qm = masked(q, h)
                    near = causal(nt(qm, k) * SCALE, qb * 256)
                    peak = jnp.max(near, axis=-1, keepdims=True)
                    if remote:
                        all_keys = rows(s * 512, 512)
                        far = nt(qm, kvr[all_keys, 0:128]) * SCALE
                        peak = jnp.maximum(peak, jnp.max(far, axis=-1, keepdims=True))
                        far = jnp.exp(far - peak)
                    near = jnp.exp(near - peak)
                    total = jnp.sum(near, axis=-1, keepdims=True)
                    if remote:
                        total = total + jnp.sum(far, axis=-1, keepdims=True)
                    inverse = 1.0 / total
                    o = nn((near * inverse).astype(BF16), v)
                    if remote:
                        o = o + nn((far * inverse).astype(BF16), kvr[all_keys, 128:256])
                    outs.append(o)
                    lse[h, r] = peak + jnp.log(total)
                att[r] = jnp.where(head_lanes[0], outs[0], outs[1]).astype(BF16)

    pl.when(yh == 0)(functools.partial(attend, False))

    @pl.when(yh == 1)
    def _():
        links.wait(kv_slot, kvr, {"yh": 0})
        attend(True)

    w_o.gather.forward()
    w_o.gather.done()

    def halves(body):
        def run(who):
            @pl.loop(0, 2)
            def _(i):
                body(rows(who * 512 + i * 256, 256))

        return run

    @halves
    def branch_tile(r):
        part_b[r] = nt(att[r], wo[...]).astype(BF16)

    sum_b = GroupSum(ring_z, c, part_b, core_b, near_b)
    branch_tile(1 - c)
    sum_b.core_send()
    branch_tile(c)
    gather_c.done()
    sum_b.start()
    w_e.gather.forward()
    w_c.gather.forward()
    sum_b.middle()
    x_own = tok_ref[...].astype(F32)
    resid[...] = x_own + sum_b.total() + off1
    normed2, inverse2 = norm_rows(resid[...])
    h2[own] = (normed2 * gain2 + off2).astype(BF16)
    gather_h = RingGather(ring_z, h2, block, 64, partner, block_partner)
    gather_h.start()
    w_e.gather.done()
    w_c.gather.done()
    gather_h.forward()
    gather_h.done()

    hb_sum[...] = jnp.zeros_like(hb_sum)

    @halves
    def mlp_tile(r):
        p = nn(h2[r], we[...]) + hidden_bias
        square = p * p
        t = jnp.tanh(GELU_COEF * (p + CUBIC * p * square))
        hid[r] = (0.5 * p * (1.0 + t)).astype(BF16)
        slope = 0.5 * (1.0 + t) + 0.5 * p * (1.0 - t * t) * (GELU_COEF * (1.0 + 3.0 * CUBIC * square))
        g = (nn(cotg[r], wc[...]) * slope).astype(BF16)
        gp[r] = g
        hb_sum[...] += jnp.sum(g.astype(F32), axis=0, keepdims=True)
        part_2[r] = nt(g, we[...]).astype(BF16)

    sum_2 = GroupSum(ring_z, c, part_2, core_2, near_2)
    mlp_tile(1 - c)
    sum_2.core_send()
    mlp_tile(c)
    sum_2.start()

    def weight_grad(out, left, right):
        @pl.loop(0, 4)
        def _(i):
            r = rows(i * 256, 256)
            out[r] = tn(left[:, r], right[...]).astype(BF16)

    g_e = WeightSum(ring_x, me, ge, 64, land_e, landy_e)
    g_c = WeightSum(ring_x, me, gc, 64, land_c, landy_c)
    weight_grad(ge, h2, gp)
    g_e.start()
    sum_2.middle()
    weight_grad(gc, cotg, hid)
    g_c.start()

    grad2 = sum_2.total()
    cot_own = cot_ref[...].astype(F32)
    gres[...] = cot_own + norm_back(grad2, normed2, inverse2, gain2)
    grad_branch = gres[...].astype(BF16)
    gbg[own] = grad_branch
    gather_b = RingGather(ring_z, gbg, block, 64, partner, block_partner)
    gather_b.start()
    vec[1:2] = jnp.sum(grad2 * normed2, axis=0, keepdims=True)
    vec[3:4] = jnp.sum(grad_branch.astype(F32), axis=0, keepdims=True)
    vec[4:5] = jnp.sum(grad2, axis=0, keepdims=True)
    vec[5:6] = jnp.sum(cot_own, axis=0, keepdims=True)
    g_e.middle()

    @halves
    def out_tile(r):
        part_o[r] = nt(hid[r], wc[...]).astype(BF16)

    sum_o = GroupSum(ring_z, c, part_o, core_o, near_o)
    gather_b.forward()
    out_tile(1 - c)
    sum_o.core_send()
    out_tile(c)
    gather_b.done()
    sum_o.start()

    @pl.loop(0, 4)
    def _(i):
        r = rows(i * 256, 256)
        gatt[r] = nn(gbg[r], wo[...]).astype(BF16)

    gkv_slot = links.slots(1)

    def attend_back(remote):
        @pl.loop(0, 2)
        def _(s):
            dk_acc[...] = jnp.zeros_like(dk_acc)
            dv_acc[...] = jnp.zeros_like(dv_acc)
            if remote:
                dk0_acc[...] = jnp.zeros_like(dk0_acc)
                dv0_acc[...] = jnp.zeros_like(dv0_acc)
            seq = rows(s * 512, 512)
            for qb in range(2):
                nk = 256 * (qb + 1)
                r = rows(s * 512 + qb * 256, 256)
                keys = rows(s * 512, nk, 512)
                q, k, v, g = qkv[r, 0:128], qkv[keys, 128:256], qkv[keys, 256:384], gatt[r]
                outs = []
                for h in range(2):
                    qm, gm, sums = masked(q, h), masked(g, h), lse[h, r]
                    near = jnp.exp(causal(nt(qm, k) * SCALE, qb * 256) - sums)
                    near_g = nt(gm, v)
                    dot = jnp.sum(near * near_g, axis=-1, keepdims=True)
                    if remote:
                        k0, v0 = kvr[seq, 0:128], kvr[seq, 128:256]
                        far = jnp.exp(nt(qm, k0) * SCALE - sums)
                        far_g = nt(gm, v0)
                        dot = dot + jnp.sum(far * far_g, axis=-1, keepdims=True)
                        far_s = (far * (far_g - dot)).astype(BF16)
                        dk0_acc[...] += tn(far_s, qm)
                        dv0_acc[...] += tn(far.astype(BF16), gm)
                    near_s = (near * (near_g - dot)).astype(BF16)
                    dk_acc[0:nk] += tn(near_s, qm)
                    dv_acc[0:nk] += tn(near.astype(BF16), gm)
                    o = nn(near_s, k)
                    if remote:
                        o = o + nn(far_s, k0)
                    outs.append(o)
                gqkv[r, 0:128] = (jnp.where(head_lanes[0], outs[0], outs[1]) * SCALE).astype(BF16)
            gqkv[seq, 128:256] = (dk_acc[...] * SCALE).astype(BF16)
            gqkv[seq, 256:384] = dv_acc[...].astype(BF16)
            if remote:
                gkv_out[seq, 0:128] = (dk0_acc[...] * SCALE).astype(BF16)
                gkv_out[seq, 128:256] = dv0_acc[...].astype(BF16)

    pl.when(yh == 0)(functools.partial(attend_back, False))
    pl.when(yh == 1)(functools.partial(attend_back, True))
    links.send_if(yh == 1, gkv_out, gkv_in, gkv_slot, {"yh": 0})
    sum_o.middle()
    g_c.middle()
    g_e.start_y()
    out_ref[...] = (resid[...] + sum_o.total() + off3).astype(BF16)
    weight_grad(go, gbg, att)
    g_o = WeightSum(ring_x, me, go, 64, land_o, landy_o)
    g_o.start()

    @pl.when(yh == 0)
    def _():
        links.wait(gkv_slot, gkv_in, {"yh": 1})
        for k in range(4):
            r = pl.ds(k * 256, 256)
            gqkv[r, 128:384] = (gqkv[r, 128:384].astype(F32) + gkv_in[r].astype(F32)).astype(BF16)

    @halves
    def grad1_tile(r):
        part_1[r] = nt(gqkv[r], wi[...]).astype(BF16)

    sum_1 = GroupSum(ring_z, c, part_1, core_1, near_1)
    grad1_tile(1 - c)
    sum_1.core_send()
    grad1_tile(c)
    sum_1.start()
    weight_grad(gi, h1, gqkv)
    g_i = WeightSum(ring_x, me, gi, 64, land_i, landy_i)
    g_i.start()
    g_c.start_y()
    g_o.middle()
    sum_1.middle()
    head_sums = jnp.sum(gqkv[...].astype(F32), axis=0, keepdims=True)
    normed1, inverse1 = norm_rows(x_own)
    grad1 = sum_1.total()
    vec[0:1] = jnp.sum(grad1 * normed1, axis=0, keepdims=True)
    vec[2:3] = jnp.sum(grad1, axis=0, keepdims=True)
    hb = hb_sum[...]
    vec[6:7] = jnp.concatenate([hb[:, 128 * (k // 2) : 128 * (k // 2) + 128] for k in range(8)], axis=1)
    vec[7:8] = jnp.concatenate([head_sums[:, 0:128]] * 8, axis=1)
    vec[8:9] = jnp.concatenate([head_sums[:, 256:384]] * 8, axis=1)
    vec[9:16] = jnp.zeros((7, 1024), F32)
    for k in range(16):
        gs[pl.ds(16 * k, 16)] = vec[:, 128 * (k // 2) : 128 * (k // 2) + 128].astype(BF16)
    g_s = WeightSum(ring_x, me, gs, 16, land_s, landy_s)
    g_s.start()
    gtok_ref[...] = gres[...] + norm_back(grad1, normed1, inverse1, gain1)
    g_s.middle()
    g_i.middle()
    g_s.start_y()
    g_o.start_y()
    g_i.start_y()
    tile = g_s.finish()
    slot = yh * 4 + z
    tens[rows(slot * 16, 16)] = tile
    mine = tens.at[rows(slot * 16, 16)]
    t_ids = links.slots(8)
    others = [(dh, dz) for dh in range(2) for dz in range(4) if dh or dz]
    for dh, dz in others:
        links.send(mine, mine, t_ids + slot, {"yh": lax.rem(yh + dh, 2), "z": lax.rem(z + dz, 4)})
    gwe_ref[...] = g_e.finish()
    gwc_ref[...] = g_c.finish()
    gwo_ref[...] = g_o.finish()
    gwi_ref[...] = g_i.finish()
    for dh, dz in others:
        theirs = lax.rem(yh + dh, 2) * 4 + lax.rem(z + dz, 4)
        ref = tens.at[rows(theirs * 16, 16)]
        links.wait(t_ids + theirs, ref, {"yh": lax.rem(yh + dh, 2), "z": lax.rem(z + dz, 4)})
    total = tens[0:16]
    for k in range(1, 8):
        total = total + tens[16 * k : 16 * k + 16]
    gsm_ref[0:6] = total[0:6]
    gsm_ref[6:16] = tile[6:16]
    links.drain()


def on_lanes(value, lane0, width):
    padded = jnp.zeros((value.shape[0], width), value.dtype)
    return lax.dynamic_update_slice(padded, value, (0, lane0))


def per_device(tokens, input_proj, output_proj, expand_proj, contract_proj, head_bias, hidden_bias, norm_gains, offsets, cotangent):
    c = lax.axis_index("c")
    dp = lax.axis_index("x") * 4 + lax.axis_index("yl") * 2 + c
    sm = jnp.concatenate(
        [
            on_lanes(jnp.concatenate([norm_gains, offsets], axis=0), c * 64, 128),
            on_lanes(hidden_bias, lax.rem(dp, 4) * 32, 128),
            on_lanes(head_bias[:, 0, :], dp * 8, 128),
            jnp.zeros((7, 128), BF16),
        ],
        axis=0,
    )
    wi = jnp.swapaxes(input_proj, 0, 1).reshape(64, 384)
    vmem = pl.BlockSpec(memory_space=pltpu.VMEM)
    shape = jax.ShapeDtypeStruct
    widths = (384, 128, 512, 512)

    def buf(r, n, t=BF16):
        return pltpu.VMEM((r, n), t)

    scratch = [buf(1024, 1024) for _ in range(5)]
    scratch += [buf(1024, n) for n in widths] + [buf(256, 128)]
    scratch += [buf(1024, n) for n in widths] + [buf(256, 128)]
    scratch += [buf(768, n) for n in widths] + [buf(192, 128)]
    scratch += [buf(256, n) for n in widths] + [buf(64, 128)]
    scratch += [buf(1024, 1024) for _ in range(4)] + [buf(512, 1024) for _ in range(4)]
    scratch += [buf(384, 1024) for _ in range(4)]
    scratch += [buf(1024, 384), buf(1024, 384), buf(1024, 256), buf(1024, 256), buf(1024, 256)]
    scratch += [buf(1024, 128), buf(1024, 128), buf(1024, 512), buf(1024, 512)]
    scratch += [pltpu.VMEM((2, 1024, 1), F32)] + [buf(512, 128, F32) for _ in range(4)]
    scratch += [buf(128, 1024, F32), buf(128, 1024, F32), buf(16, 1024, F32), buf(128, 128, F32)]
    scratch += [buf(1, 512, F32)]
    scratch += [pltpu.SemaphoreType.DMA((N_SEMS,)), pltpu.SemaphoreType.DMA((N_SEMS,))]
    out, gtok, gwi, gwo, gwe, gwc, gsm = pl.pallas_call(
        layer_kernel,
        out_shape=(
            shape((128, 1024), BF16),
            shape((128, 1024), F32),
            *(shape((64, n), F32) for n in widths),
            shape((16, 128), F32),
        ),
        in_specs=[vmem] * 7,
        out_specs=[vmem] * 7,
        scratch_shapes=scratch,
        compiler_params=pltpu.CompilerParams(
            collective_id=0, has_side_effects=True, vmem_limit_bytes=58 * 1024 * 1024
        ),
    )(tokens, cotangent, wi, output_proj.T, expand_proj, contract_proj.T, sm)
    grad_input = jnp.swapaxes(gwi.reshape(64, 3, 128), 0, 1)
    mine = lax.dynamic_slice(gsm, (0, c * 64), (6, 64))
    grad_hidden = lax.dynamic_slice(gsm, (6, lax.rem(dp, 4) * 32), (1, 32))
    grad_head = lax.dynamic_slice(gsm, (7, dp * 8), (2, 8))[:, None, :]
    return (out, gtok, grad_input, gwo.T, gwe, gwc.T, grad_head, grad_hidden, mine[0:2], mine[2:6])


def solution(mesh):
    split = Mesh(mesh.devices.reshape(4, 2, 2, 2, 4), ("x", "yl", "c", "yh", "z"))
    token_rows = P(DP + TENSOR, None)
    weights = (
        P(None, DP, TENSOR),
        P(TENSOR, DP),
        P(DP, TENSOR),
        P(TENSOR, DP),
        P(None, TENSOR, DP),
        P(TENSOR, DP),
        P(None, DP),
        P(None, DP),
    )
    return jax.shard_map(
        per_device,
        mesh=split,
        in_specs=(token_rows, *weights, token_rows),
        out_specs=(token_rows, token_rows, *weights),
        check_vma=False,
    )
```

time: 667 us -> 173 us (0.26)
  waiting for transfers between devices: 325 us -> 0 us
  blocking collectives: 161 us -> 0 us
  Pallas kernels: 0 us -> 157 us
  starting transfers between devices: 52.3 us -> 0 us
  matrix products: 48.7 us -> 0 us
  other arithmetic: 33 us -> 0.68 us
  between operations: 16.8 us -> 0.76 us
  local copies, waits for them, and re-layouts: 28.7 us -> 13.7 us
    reduce_scatter x4 -> x0, waiting for transfers between devices: 229 us -> none  [the longest x1 83.4 us: per_device(): lax.psum_scatter(jnp.dot(piece, full_output, preferred_element_type=jnp.f...]
    pallas_call x0 -> x1, Pallas kernels: none -> 157 us  [per_device(): pl.pallas_call(layer_kernel, out_shape=(shape((128, 1024), BF16), shape((...]
    all_to_all x12 -> x0, waiting for transfers between devices: 95.5 us -> none  [the longest x5 61.6 us: sent_to_all(): lax.all_to_all(jnp.broadcast_to(value[None], (devices, *value.shape)), ax...]
    all_gather x4 -> x0, blocking collectives: 93.4 us -> none  [the longest x1 35.4 us: per_device(): lax.all_gather(head_bias, DP, axis=2, tiled=True)]
    all_to_all x12 -> x0, starting transfers between devices: 51.8 us -> none  [the longest x5 26.2 us: sent_to_all(): lax.all_to_all(jnp.broadcast_to(value[None], (devices, *value.shape)), ax...]
    dot_general x24 -> x0, matrix products: 48.7 us -> none  [the longest x1 6.01 us: per_device(): jnp.einsum('td,hd->th', grad_rows, back_contract, preferred_element_type=...]
    unnamed x1 -> x0, blocking collectives: 38.6 us -> none
    all_to_all x7 -> x0, blocking collectives: 28.5 us -> none  [sent_and_summed(): lax.all_to_all(in_blocks(value, dim, devices), axis, 0, 0, tiled=True)]
  transfers between devices with their start and end apart: 18 -> 0, of which waited for: 13 -> 0; matrix products, arithmetic and copies ran while one was open for 8% -> 0% of each run, Pallas kernels for 0% -> 0%
where the time goes in v1:
time: 173 us; the launch traced here: 172 us
  Pallas kernels  157 us (91%)
  local copies, waits for them, and re-layouts  13.7 us (8%)
    pallas_call x1, Pallas kernels, per_device(): pl.pallas_call(layer_kernel, out_shape=(shape((128, 1024), BF16), shape((...  157 us
    unnamed x24, local copies, waits for them, and re-layouts  7.24 us

profile of v1, /device:TPU:0, one launch (start us, length us, event | category | flops | bytes accessed | tf_op | source)
XLA Modules:
  0.0 172.0 jit_solution(14130037336444117970)
XLA Ops:
  0.6 0.0 copy-start
  0.7 0.1 pad.3.clone
  0.8 0.0 copy-start.7
  0.8 0.7 copy-done.7
  1.4 0.1 dynamic_update_slice.11
  1.5 0.0 copy-start.8
  1.5 0.6 copy-done.8
  2.2 0.1 dynamic_update_slice.10
  2.2 0.6 copy-done.5
  2.8 0.0 copy-done.6
  2.9 0.1 dynamic_update_slice.9
  3.0 0.7 maximum_maximum_fusion.sm_ref
  3.7 0.0 copy-done
  3.7 0.6 copy_bitcast_fusion.wi_ref
  4.3 156.8 %shard_map.177 = (bf16[128,1024]{1,0:T(8,128)(2,1)}, f32[128,1024]{1,0:T(8,128)}, f32[64,384]{1,0:T(8,128)}, f32[64,128]{1,0:T(8,128)}, f32[64,512]{1,0:T(8,128)}, /*index=5*/f32[64,512]{1,0:T(8,128)}, f32[16,128]{1,0:T(8,128)}) custom-call(bf16[128,1024]{1,0:T(8,128)(2,1)} %tok_ref.1, bf16[128,1024]{1,0:T(8,128)(2,1)} %cot_ref.1, ...), custom_call_target="tpu_custom_call" | custom-call | tf_op jit(solution)/shard_map/pallas_call | solution.py:715
  161.1 0.0 copy-start.1
  161.2 1.3 constant_dynamic-slice_fusion
  162.5 1.3 constant_dynamic-slice_fusion.1
  163.8 0.7 constant_dynamic-slice_fusion.2
  164.5 0.6 slice.6
  165.1 0.6 slice.7
  165.7 0.9 reshape.27
  166.6 0.6 copy.24
  167.3 1.7 copy.36
  168.9 0.0 copy-done.1
  169.0 0.8 copy.37
  169.7 0.0 copy-done.4
  169.7 0.6 copy.38
  170.4 0.0 copy-done.3
  170.4 0.7 copy.39
  171.0 0.3 copy-done.2
  171.3 0.7 copy.40
  (10 shorter events, 0.0 us)
Async XLA Ops:
  0.6 3.0 %copy-start = (bf16[3,64,128]{2,1,0:T(8,128)(2,1)S(1)}, bf16[3,64,128]{2,1,0:T(8,128)(2,1)}, u32[]{:S(2)}) copy-start(bf16[3,64,128]{2,1,0:T(8,128)(2,1)} %param.11) | copy-start | bytes 147460
  0.8 0.7 copy-start.7
  1.5 0.7 copy-start.8
  2.2 0.7 copy-start.5
  2.2 0.7 copy-start.6
  161.1 7.8 %copy-start.1 = (f32[128,1024]{1,0:T(8,128)S(1)}, f32[128,1024]{1,0:T(8,128)}, u32[]{:S(2)}) copy-start(f32[128,1024]{1,0:T(8,128)} %get-tuple-element.55) | copy-start | bytes 1572868
  168.9 0.8 copy-start.4
  168.9 1.4 copy-start.3
  170.4 1.0 copy-start.2

commit v2 on v1

--- a/solution.py
+++ b/solution.py
@@ -55,6 +55,12 @@
     def __init__(self, send_sems, recv_sems):
         self.send_sems, self.recv_sems = send_sems, recv_sems
         self.sent, self.received, self.open = 0, 0, []
+
+    def outgoing(self, count):
+        first = self.sent
+        self.sent += count
+        assert self.sent <= N_SEMS
+        return first
 
     def slots(self, count):
         first = self.received
@@ -227,18 +233,38 @@
         self.links, self.c, self.buf, self.from_core = ring.links, c, buf, from_core
         self.partner = {"c": 1 - c}
         self.order = (ring.far, ring.right, ring.left, ring.pos)
-        self.ids = ring.links.slots(4)
+        self.ids, self.out_ids = ring.links.slots(4), ring.links.outgoing(4)
         self.sum = RingSum(ring, buf, lambda p: c * 512 + p * 128, 64, land)
 
-    def core_send(self):
-        for k, pos in enumerate(self.order):
-            src = self.buf.at[rows((1 - self.c) * 512 + pos * 128, 128)]
-            dst = self.from_core.at[rows(pos * 128, 128)]
-            self.links.send(src, dst, self.ids + k, self.partner)
+    def core_copy(self, pos):
+        return pltpu.make_async_remote_copy(
+            src_ref=self.buf.at[rows((1 - self.c) * 512 + pos * 128, 128)],
+            dst_ref=self.from_core.at[rows(pos * 128, 128)],
+            send_sem=self.links.send_sems.at[self.out_ids + pos],
+            recv_sem=self.links.recv_sems.at[self.ids + pos],
+            device_id=self.partner,
+            device_id_type=MESH,
+        )
+
+    def run(self, body):
+        first = self.order[0] // 2
+
+        @pl.loop(0, 4)
+        def _(i):
+            tile = lax.rem(first + i, 2)
+            body(rows(lax.rem(1 - self.c + i // 2, 2) * 512 + tile * 256, 256))
+
+            @pl.when(i < 2)
+            def _():
+                self.core_copy(tile * 2).start()
+                self.core_copy(tile * 2 + 1).start()
+
+        for pos in range(4):
+            self.links.open.append((None, self.core_copy(pos)))
 
     def core_add(self, k):
         got = self.from_core.at[rows(self.order[k] * 128, 128)]
-        self.links.wait(self.ids + k, got, self.partner)
+        self.links.wait(self.ids + self.order[k], got, self.partner)
         ref = self.buf.at[rows(self.c * 512 + self.order[k] * 128, 128)]
         ref[...] = (ref[...].astype(F32) + got[...].astype(F32)).astype(BF16)
 
@@ -296,10 +322,13 @@
     def middle(self):
         self.sum.middle()
 
+    def x_total(self):
+        return self.sum.total()
+
     def start_y(self):
         x, yl, c, yh, z = self.me
         links, size = self.ring.links, self.size
-        total = self.sum.total()
+        total = self.x_total()
         self.buf[rows(x * 4 * size, 4 * size)] = total.astype(BF16)
         slot = yh * 2 + yl
         dst = self.land_y.at[rows(slot * size, size)]
@@ -322,16 +351,43 @@
         return total
 
 
+class SmallSum(WeightSum):
+    def __init__(self, ring, me, buf, size, land, land_y):
+        self.ring, self.me, self.buf, self.size = ring, me, buf, size
+        self.land, self.land_y = land, land_y
+        self.x_ids = ring.links.slots(4)
+        self.ids = ring.links.slots(4)
+
+    def start(self):
+        x = self.me[0]
+        for d in (2, 1, 3):
+            to = lax.rem(x + d, 4)
+            src = self.buf.at[rows(to * 4 * self.size, 4 * self.size)]
+            dst = self.land.at[pl.ds(d * 4 * self.size, 4 * self.size)]
+            self.ring.links.send(src, dst, self.x_ids + d, {"x": to})
+
+    def x_total(self):
+        x = self.me[0]
+        total = self.buf[rows(x * 4 * self.size, 4 * self.size)].astype(F32)
+        for d in (1, 3, 2):
+            ref = self.land.at[pl.ds(d * 4 * self.size, 4 * self.size)]
+            self.ring.links.wait(self.x_ids + d, ref, {"x": lax.rem(x + 4 - d, 4)})
+            total = total + ref[...].astype(F32)
+        return total
+
+
 def layer_kernel(
-    tok_ref, cot_ref, wi_ref, wo_ref, we_ref, wc_ref, sm_ref,
+    tok_ref, cot_ref, wi_ref, wo_ref, we_ref, wc_ref, gain_ref, off_ref, hid_ref, head_ref,
     out_ref, gtok_ref, gwi_ref, gwo_ref, gwe_ref, gwc_ref, gsm_ref,
     xg, cotg, h1, h2, gbg, wi, wo, we, wc, sm, gi, go, ge, gc, gs,
     land_i, land_o, land_e, land_c, land_s, landy_i, landy_o, landy_e, landy_c, landy_s,
     part_b, part_o, part_2, part_1, core_b, core_o, core_2, core_1, near_b, near_o, near_2, near_1,
     qkv, gqkv, kvr, gkv_out, gkv_in, att, gatt, hid, gp, lse, dk_acc, dv_acc, dk0_acc, dv0_acc,
-    resid, gres, vec, tens, hb_sum, send_sems, recv_sems,
+    resid, gres, vec, tens, hb_sum, wi_own, sm_own, sm_parts, top, low_sum, att_f, gq_f, delta, columns,
+    vec_t, send_sems, recv_sems, local_sems,
 ):
     x, yl, c, yh, z = me = tuple(lax.axis_index(a) for a in ("x", "yl", "c", "yh", "z"))
+    dp = x * 4 + yl * 2 + c
     links = Links(send_sems, recv_sems)
     ring_z, ring_x = Ring(links, "z", z), Ring(links, "x", x)
     partner = {"c": 1 - c}
@@ -342,8 +398,16 @@
     def block_partner(p):
         return (1 - c) * 512 + p * 128
 
+    own = rows(block(z), 128)
+    loads = [pltpu.make_async_copy(tok_ref, xg.at[own], local_sems.at[0])]
+    loads.append(pltpu.make_async_copy(cot_ref, cotg.at[own], local_sems.at[1]))
+    for k in range(3):
+        loads.append(pltpu.make_async_copy(wi_ref.at[k], wi_own.at[:, pl.ds(128 * k, 128)], local_sems.at[2 + k]))
+    for load in loads:
+        load.start()
+
     barrier = pltpu.get_barrier_semaphore()
-    peers = [{"x": ring_x.right}, {"x": ring_x.left}]
+    peers = [{"x": ring_x.right}, {"x": ring_x.left}, {"x": ring_x.far}]
     for dh in range(2):
         for dz in range(4):
             if dh or dz:
@@ -355,22 +419,33 @@
                     peers.append({"yl": lax.rem(yl + dl, 2), "c": lax.rem(c + dc, 2), "yh": lax.rem(yh + dh, 2)})
     for peer in peers:
         pl.semaphore_signal(barrier, inc=1, device_id=peer, device_id_type=MESH)
-    own = rows(block(z), 128)
-    xg[own] = tok_ref[...]
-    cotg[own] = cot_ref[...]
+    sm_parts[...] = jnp.zeros_like(sm_parts)
+    sm_parts[0:2, 0:64] = gain_ref[...].astype(F32)
+    sm_parts[2:6, 0:64] = off_ref[...].astype(F32)
+    sm_parts[22:23, 0:32] = hid_ref[...].astype(F32)
+    sm_parts[39:40, 0:8] = head_ref[0].astype(F32)
+    sm_parts[40:41, 0:8] = head_ref[1].astype(F32)
+    placed = pltpu.roll(sm_parts[0:16], c * 64, 1) + pltpu.roll(sm_parts[16:32], lax.rem(dp, 4) * 32, 1)
+    sm_own[...] = (placed + pltpu.roll(sm_parts[32:48], dp * 8, 1)).astype(BF16)
+    for load in loads:
+        load.wait()
     pl.semaphore_wait(barrier, len(peers))
 
-    gather_x = RingGather(ring_z, xg, block, 64, partner, block_partner)
-    gather_x.start()
-    w_sm = WeightGather(ring_x, me, sm, 16, sm_ref)
-    w_i = WeightGather(ring_x, me, wi, 64, wi_ref)
+    w_sm = WeightGather(ring_x, me, sm, 16, sm_own)
+    w_i = WeightGather(ring_x, me, wi, 64, wi_own)
     w_o = WeightGather(ring_x, me, wo, 64, wo_ref)
     w_e = WeightGather(ring_x, me, we, 64, we_ref)
     w_c = WeightGather(ring_x, me, wc, 64, wc_ref)
-    for w in (w_sm, w_i, w_o, w_e, w_c):
-        w.start()
+    w_sm.start()
+    w_i.start()
+    gather_x = RingGather(ring_z, xg, block, 64, partner, block_partner)
+    gather_x.start()
+    w_o.start()
     w_sm.start_x()
     w_i.start_x()
+    w_o.start_x()
+    w_e.start()
+    w_c.start()
     gather_x.forward()
     w_sm.gather.forward()
     w_i.gather.forward()
@@ -390,19 +465,29 @@
     gain1, gain2 = gains[0:1], gains[1:2]
     off0, off1, off2, off3 = (offs[k : k + 1] for k in range(4))
 
-    w_i.gather.done()
-
     @pl.loop(0, 4)
     def _(i):
         r = rows(i * 256, 256)
         normed, _ = norm_rows(xg[r].astype(F32))
-        low = (normed * gain1 + off0).astype(BF16)
-        h1[r] = low
-        qkv[r] = (nn(low, wi[...]) + qkv_bias).astype(BF16)
-
-    kv_slot = links.slots(1)
-    links.send_if(yh == 0, qkv.at[:, pl.ds(128, 256)], kvr, kv_slot, {"yh": 1})
-    w_o.start_x()
+        h1[r] = (normed * gain1 + off0).astype(BF16)
+
+    w_i.gather.done()
+    w_o.gather.forward()
+
+    kv_slots = links.slots(2)
+    kv_copies = []
+    for s in range(2):
+        part = pl.ds(s * 512, 512)
+        kv_copies.append(links.make(qkv.at[part, pl.ds(128, 256)], kvr.at[part], kv_slots + s, {"yh": 1}))
+        links.open.append((yh == 0, kv_copies[s]))
+
+    @pl.loop(0, 4)
+    def _(i):
+        r = rows(i * 256, 256)
+        qkv[r] = (nn(h1[r], wi[...]) + qkv_bias).astype(BF16)
+        for s in range(2):
+            pl.when((i == 2 * s + 1) & (yh == 0))(kv_copies[s].start)
+
     w_e.start_x()
     w_c.start_x()
     gather_c.forward()
@@ -417,7 +502,7 @@
     def masked(value, h):
         return jnp.where(head_lanes[h], value, jnp.zeros_like(value))
 
-    def attend(remote):
+    def attend():
         @pl.loop(0, 2)
         def _(s):
             for qb in range(2):
@@ -427,58 +512,58 @@
                 q, k, v = qkv[r, 0:128], qkv[keys, 128:256], qkv[keys, 256:384]
                 outs = []
                 for h in range(2):
-                    qm = masked(q, h)
-                    near = causal(nt(qm, k) * SCALE, qb * 256)
+                    near = causal(nt(masked(q, h), k) * SCALE, qb * 256)
                     peak = jnp.max(near, axis=-1, keepdims=True)
-                    if remote:
-                        all_keys = rows(s * 512, 512)
-                        far = nt(qm, kvr[all_keys, 0:128]) * SCALE
-                        peak = jnp.maximum(peak, jnp.max(far, axis=-1, keepdims=True))
-                        far = jnp.exp(far - peak)
                     near = jnp.exp(near - peak)
-                    total = jnp.sum(near, axis=-1, keepdims=True)
-                    if remote:
-                        total = total + jnp.sum(far, axis=-1, keepdims=True)
-                    inverse = 1.0 / total
-                    o = nn((near * inverse).astype(BF16), v)
-                    if remote:
-                        o = o + nn((far * inverse).astype(BF16), kvr[all_keys, 128:256])
-                    outs.append(o)
-                    lse[h, r] = peak + jnp.log(total)
-                att[r] = jnp.where(head_lanes[0], outs[0], outs[1]).astype(BF16)
-
-    pl.when(yh == 0)(functools.partial(attend, False))
+                    top[h, r] = peak
+                    low_sum[h, r] = jnp.sum(near, axis=-1, keepdims=True)
+                    outs.append(nn(near.astype(BF16), v))
+                att_f[r] = jnp.where(head_lanes[0], outs[0], outs[1])
+
+    def finish(remote):
+        @pl.loop(0, 4)
+        def _(i):
+            r = rows(i * 256, 256)
+            keys = rows((i // 2) * 512, 512)
+            outs = []
+            for h in range(2):
+                peak, total, o = top[h, r], low_sum[h, r], att_f[r]
+                if remote:
+                    far = nt(masked(qkv[r, 0:128], h), kvr[keys, 0:128]) * SCALE
+                    higher = jnp.maximum(peak, jnp.max(far, axis=-1, keepdims=True))
+                    far = jnp.exp(far - higher)
+                    shrink = jnp.exp(peak - higher)
+                    total = total * shrink + jnp.sum(far, axis=-1, keepdims=True)
+                    o = o * shrink + nn(far.astype(BF16), kvr[keys, 128:256])
+                    peak = higher
+                outs.append(o * (1.0 / total))
+                lse[h, r] = peak + jnp.log(total)
+            o = jnp.where(head_lanes[0], outs[0], outs[1])
+            att_f[r] = o
+            att[r] = o.astype(BF16)
+
+    attend()
+    w_o.gather.done()
+    pl.when(yh == 0)(functools.partial(finish, False))
 
     @pl.when(yh == 1)
     def _():
-        links.wait(kv_slot, kvr, {"yh": 0})
-        attend(True)
-
-    w_o.gather.forward()
-    w_o.gather.done()
-
-    def halves(body):
-        def run(who):
-            @pl.loop(0, 2)
-            def _(i):
-                body(rows(who * 512 + i * 256, 256))
-
-        return run
-
-    @halves
+        for s in range(2):
+            links.wait(kv_slots + s, kvr.at[pl.ds(s * 512, 512)], {"yh": 0})
+        finish(True)
+
     def branch_tile(r):
         part_b[r] = nt(att[r], wo[...]).astype(BF16)
 
     sum_b = GroupSum(ring_z, c, part_b, core_b, near_b)
-    branch_tile(1 - c)
-    sum_b.core_send()
-    branch_tile(c)
+    sum_b.run(branch_tile)
     gather_c.done()
     sum_b.start()
     w_e.gather.forward()
     w_c.gather.forward()
     sum_b.middle()
-    x_own = tok_ref[...].astype(F32)
+    x_own = xg[own].astype(F32)
+    cot_own = cotg[own].astype(F32)
     resid[...] = x_own + sum_b.total() + off1
     normed2, inverse2 = norm_rows(resid[...])
     h2[own] = (normed2 * gain2 + off2).astype(BF16)
@@ -486,12 +571,12 @@
     gather_h.start()
     w_e.gather.done()
     w_c.gather.done()
+    vec_t[...] = jnp.transpose(vectors)
     gather_h.forward()
     gather_h.done()
 
     hb_sum[...] = jnp.zeros_like(hb_sum)
 
-    @halves
     def mlp_tile(r):
         p = nn(h2[r], we[...]) + hidden_bias
         square = p * p
@@ -504,9 +589,7 @@
         part_2[r] = nt(g, we[...]).astype(BF16)
 
     sum_2 = GroupSum(ring_z, c, part_2, core_2, near_2)
-    mlp_tile(1 - c)
-    sum_2.core_send()
-    mlp_tile(c)
+    sum_2.run(mlp_tile)
     sum_2.start()
 
     def weight_grad(out, left, right):
@@ -524,7 +607,6 @@
     g_c.start()
 
     grad2 = sum_2.total()
-    cot_own = cot_ref[...].astype(F32)
     gres[...] = cot_own + norm_back(grad2, normed2, inverse2, gain2)
     grad_branch = gres[...].astype(BF16)
     gbg[own] = grad_branch
@@ -536,33 +618,65 @@
     vec[5:6] = jnp.sum(cot_own, axis=0, keepdims=True)
     g_e.middle()
 
-    @halves
     def out_tile(r):
         part_o[r] = nt(hid[r], wc[...]).astype(BF16)
 
     sum_o = GroupSum(ring_z, c, part_o, core_o, near_o)
     gather_b.forward()
-    out_tile(1 - c)
-    sum_o.core_send()
-    out_tile(c)
+    sum_o.run(out_tile)
     gather_b.done()
     sum_o.start()
+    g_c.middle()
 
     @pl.loop(0, 4)
     def _(i):
         r = rows(i * 256, 256)
-        gatt[r] = nn(gbg[r], wo[...]).astype(BF16)
-
-    gkv_slot = links.slots(1)
-
-    def attend_back(remote):
+        g = nn(gbg[r], wo[...])
+        low = g.astype(BF16)
+        gatt[r] = low
+        product = low.astype(F32) * att_f[r]
+        for h in range(2):
+            delta[h, r] = jnp.sum(masked(product, h), axis=-1, keepdims=True)
+
+    gkv_slots = links.slots(2)
+    gkv_copies = []
+    for s in range(2):
+        part = pl.ds(s * 512, 512)
+        gkv_copies.append(links.make(gkv_out.at[part], gkv_in.at[part], gkv_slots + s, {"yh": 0}))
+        links.open.append((yh == 1, gkv_copies[s]))
+
+    def attend_far():
+        @pl.loop(0, 2)
+        def _(s):
+            seq = rows(s * 512, 512)
+            k, v = kvr[seq, 0:128], kvr[seq, 128:256]
+            dk0_acc[...] = jnp.zeros_like(dk0_acc)
+            dv0_acc[...] = jnp.zeros_like(dv0_acc)
+
+            @pl.loop(0, 2)
+            def _(qb):
+                r = rows(s * 512 + qb * 256, 256)
+                q, g = qkv[r, 0:128], gatt[r]
+                outs = []
+                for h in range(2):
+                    qm, gm = masked(q, h), masked(g, h)
+                    far = jnp.exp(nt(qm, k) * SCALE - lse[h, r])
+                    far_s = (far * (nt(gm, v) - delta[h, r])).astype(BF16)
+                    dk0_acc[...] += tn(far_s, qm)
+                    dv0_acc[...] += tn(far.astype(BF16), gm)
+                    outs.append(nn(far_s, k))
+                gq_f[r] = jnp.where(head_lanes[0], outs[0], outs[1])
+
+            gkv_out[seq, 0:128] = (dk0_acc[...] * SCALE).astype(BF16)
+            gkv_out[seq, 128:256] = dv0_acc[...].astype(BF16)
+            for k in range(2):
+                pl.when(s == k)(gkv_copies[k].start)
+
+    def attend_back():
         @pl.loop(0, 2)
         def _(s):
             dk_acc[...] = jnp.zeros_like(dk_acc)
             dv_acc[...] = jnp.zeros_like(dv_acc)
-            if remote:
-                dk0_acc[...] = jnp.zeros_like(dk0_acc)
-                dv0_acc[...] = jnp.zeros_like(dv0_acc)
             seq = rows(s * 512, 512)
             for qb in range(2):
                 nk = 256 * (qb + 1)
@@ -571,70 +685,64 @@
                 q, k, v, g = qkv[r, 0:128], qkv[keys, 128:256], qkv[keys, 256:384], gatt[r]
                 outs = []
                 for h in range(2):
-                    qm, gm, sums = masked(q, h), masked(g, h), lse[h, r]
-                    near = jnp.exp(causal(nt(qm, k) * SCALE, qb * 256) - sums)
-                    near_g = nt(gm, v)
-                    dot = jnp.sum(near * near_g, axis=-1, keepdims=True)
-                    if remote:
-                        k0, v0 = kvr[seq, 0:128], kvr[seq, 128:256]
-                        far = jnp.exp(nt(qm, k0) * SCALE - sums)
-                        far_g = nt(gm, v0)
-                        dot = dot + jnp.sum(far * far_g, axis=-1, keepdims=True)
-                        far_s = (far * (far_g - dot)).astype(BF16)
-                        dk0_acc[...] += tn(far_s, qm)
-                        dv0_acc[...] += tn(far.astype(BF16), gm)
-                    near_s = (near * (near_g - dot)).astype(BF16)
+                    qm, gm = masked(q, h), masked(g, h)
+                    near = jnp.exp(causal(nt(qm, k) * SCALE, qb * 256) - lse[h, r])
+                    near_s = (near * (nt(gm, v) - delta[h, r])).astype(BF16)
                     dk_acc[0:nk] += tn(near_s, qm)
                     dv_acc[0:nk] += tn(near.astype(BF16), gm)
-                    o = nn(near_s, k)
-                    if remote:
-                        o = o + nn(far_s, k0)
-                    outs.append(o)
-                gqkv[r, 0:128] = (jnp.where(head_lanes[0], outs[0], outs[1]) * SCALE).astype(BF16)
+                    outs.append(nn(near_s, k))
+                total = gq_f[r] + jnp.where(head_lanes[0], outs[0], outs[1])
+                gqkv[r, 0:128] = (total * SCALE).astype(BF16)
             gqkv[seq, 128:256] = (dk_acc[...] * SCALE).astype(BF16)
             gqkv[seq, 256:384] = dv_acc[...].astype(BF16)
-            if remote:
-                gkv_out[seq, 0:128] = (dk0_acc[...] * SCALE).astype(BF16)
-                gkv_out[seq, 128:256] = dv0_acc[...].astype(BF16)
-
-    pl.when(yh == 0)(functools.partial(attend_back, False))
-    pl.when(yh == 1)(functools.partial(attend_back, True))
-    links.send_if(yh == 1, gkv_out, gkv_in, gkv_slot, {"yh": 0})
-    sum_o.middle()
-    g_c.middle()
+
+    @pl.when(yh == 0)
+    def _():
+        gq_f[...] = jnp.zeros_like(gq_f)
+
+    pl.when(yh == 1)(attend_far)
     g_e.start_y()
-    out_ref[...] = (resid[...] + sum_o.total() + off3).astype(BF16)
     weight_grad(go, gbg, att)
     g_o = WeightSum(ring_x, me, go, 64, land_o, landy_o)
     g_o.start()
+    attend_back()
+    sum_o.middle()
+    g_o.middle()
 
     @pl.when(yh == 0)
     def _():
-        links.wait(gkv_slot, gkv_in, {"yh": 1})
-        for k in range(4):
-            r = pl.ds(k * 256, 256)
-            gqkv[r, 128:384] = (gqkv[r, 128:384].astype(F32) + gkv_in[r].astype(F32)).astype(BF16)
-
-    @halves
+        for s in range(2):
+            links.wait(gkv_slots + s, gkv_in.at[pl.ds(s * 512, 512)], {"yh": 1})
+
+            @pl.loop(0, 2)
+            def _(k):
+                r = rows(s * 512 + k * 256, 256)
+                gqkv[r, 128:384] = (gqkv[r, 128:384].astype(F32) + gkv_in[r].astype(F32)).astype(BF16)
+
     def grad1_tile(r):
         part_1[r] = nt(gqkv[r], wi[...]).astype(BF16)
 
     sum_1 = GroupSum(ring_z, c, part_1, core_1, near_1)
-    grad1_tile(1 - c)
-    sum_1.core_send()
-    grad1_tile(c)
+    sum_1.run(grad1_tile)
     sum_1.start()
-    weight_grad(gi, h1, gqkv)
+    head_sums = jnp.sum(gqkv[...].astype(F32), axis=0, keepdims=True)
+
+    @pl.loop(0, 4)
+    def _(i):
+        r = rows(i * 256, 256)
+        g = tn(h1[:, r], gqkv[...])
+        gi[r] = g.astype(BF16)
+        weight = wi[r].astype(F32)
+        off_grad = jnp.sum(weight * head_sums, axis=-1, keepdims=True)
+        mixed = jnp.sum(weight * g, axis=-1, keepdims=True)
+        gain_grad = (mixed - vec_t[r, 2:3] * off_grad) / vec_t[r, 0:1]
+        columns[r] = jnp.where(lane == 0, gain_grad, jnp.where(lane == 2, off_grad, 0.0))
+
     g_i = WeightSum(ring_x, me, gi, 64, land_i, landy_i)
     g_i.start()
-    g_c.start_y()
-    g_o.middle()
-    sum_1.middle()
-    head_sums = jnp.sum(gqkv[...].astype(F32), axis=0, keepdims=True)
-    normed1, inverse1 = norm_rows(x_own)
-    grad1 = sum_1.total()
-    vec[0:1] = jnp.sum(grad1 * normed1, axis=0, keepdims=True)
-    vec[2:3] = jnp.sum(grad1, axis=0, keepdims=True)
+    turned = jnp.transpose(columns[...])
+    vec[0:1] = turned[0:1]
+    vec[2:3] = turned[2:3]
     hb = hb_sum[...]
     vec[6:7] = jnp.concatenate([hb[:, 128 * (k // 2) : 128 * (k // 2) + 128] for k in range(8)], axis=1)
     vec[7:8] = jnp.concatenate([head_sums[:, 0:128]] * 8, axis=1)
@@ -642,14 +750,16 @@
     vec[9:16] = jnp.zeros((7, 1024), F32)
     for k in range(16):
         gs[pl.ds(16 * k, 16)] = vec[:, 128 * (k // 2) : 128 * (k // 2) + 128].astype(BF16)
-    g_s = WeightSum(ring_x, me, gs, 16, land_s, landy_s)
+    g_s = SmallSum(ring_x, me, gs, 16, land_s, landy_s)
     g_s.start()
-    gtok_ref[...] = gres[...] + norm_back(grad1, normed1, inverse1, gain1)
-    g_s.middle()
+    sum_1.middle()
+    g_c.start_y()
+    g_o.start_y()
+    out_ref[...] = (resid[...] + sum_o.total() + off3).astype(BF16)
+    g_s.start_y()
     g_i.middle()
-    g_s.start_y()
-    g_o.start_y()
-    g_i.start_y()
+    normed1, inverse1 = norm_rows(x_own)
+    gtok_ref[...] = gres[...] + norm_back(sum_1.total(), normed1, inverse1, gain1)
     tile = g_s.finish()
     slot = yh * 4 + z
     tens[rows(slot * 16, 16)] = tile
@@ -658,10 +768,10 @@
     others = [(dh, dz) for dh in range(2) for dz in range(4) if dh or dz]
     for dh, dz in others:
         links.send(mine, mine, t_ids + slot, {"yh": lax.rem(yh + dh, 2), "z": lax.rem(z + dz, 4)})
+    g_i.start_y()
     gwe_ref[...] = g_e.finish()
     gwc_ref[...] = g_c.finish()
     gwo_ref[...] = g_o.finish()
-    gwi_ref[...] = g_i.finish()
     for dh, dz in others:
         theirs = lax.rem(yh + dh, 2) * 4 + lax.rem(z + dz, 4)
         ref = tens.at[rows(theirs * 16, 16)]
@@ -671,27 +781,34 @@
         total = total + tens[16 * k : 16 * k + 16]
     gsm_ref[0:6] = total[0:6]
     gsm_ref[6:16] = tile[6:16]
+    gwi_ref[...] = g_i.finish()
     links.drain()
 
 
-def on_lanes(value, lane0, width):
-    padded = jnp.zeros((value.shape[0], width), value.dtype)
-    return lax.dynamic_update_slice(padded, value, (0, lane0))
-
-
-def per_device(tokens, input_proj, output_proj, expand_proj, contract_proj, head_bias, hidden_bias, norm_gains, offsets, cotangent):
+def final_kernel(
+    out_k, gtok_k, gwi, gwo, gwe, gwc, gsm,
+    out_ref, gtok_ref, gi_ref, go_ref, ge_ref, gc_ref, head_ref, hid_ref, gain_ref, off_ref,
+):
     c = lax.axis_index("c")
     dp = lax.axis_index("x") * 4 + lax.axis_index("yl") * 2 + c
-    sm = jnp.concatenate(
-        [
-            on_lanes(jnp.concatenate([norm_gains, offsets], axis=0), c * 64, 128),
-            on_lanes(hidden_bias, lax.rem(dp, 4) * 32, 128),
-            on_lanes(head_bias[:, 0, :], dp * 8, 128),
-            jnp.zeros((7, 128), BF16),
-        ],
-        axis=0,
-    )
-    wi = jnp.swapaxes(input_proj, 0, 1).reshape(64, 384)
+    out_ref[...] = out_k[...]
+    gtok_ref[...] = gtok_k[...]
+    for k in range(3):
+        gi_ref[k] = gwi[:, 128 * k : 128 * k + 128]
+    go_ref[...] = jnp.transpose(gwo[...])
+    ge_ref[...] = gwe[...]
+    gc_ref[...] = jnp.transpose(gwc[...])
+    small = gsm[...]
+    mine = pltpu.roll(small, lax.rem(128 - c * 64, 128), 1)
+    gain_ref[...] = mine[0:2, 0:64]
+    off_ref[...] = mine[2:6, 0:64]
+    hid_ref[...] = pltpu.roll(small, lax.rem(128 - lax.rem(dp, 4) * 32, 128), 1)[6:7, 0:32]
+    heads = pltpu.roll(small, lax.rem(128 - dp * 8, 128), 1)
+    head_ref[0] = heads[7:8, 0:8]
+    head_ref[1] = heads[8:9, 0:8]
+
+
+def per_device(tokens, input_proj, output_proj, expand_proj, contract_proj, head_bias, hidden_bias, norm_gains, offsets, cotangent):
     vmem = pl.BlockSpec(memory_space=pltpu.VMEM)
     shape = jax.ShapeDtypeStruct
     widths = (384, 128, 512, 512)
@@ -702,7 +819,7 @@
     scratch = [buf(1024, 1024) for _ in range(5)]
     scratch += [buf(1024, n) for n in widths] + [buf(256, 128)]
     scratch += [buf(1024, n) for n in widths] + [buf(256, 128)]
-    scratch += [buf(768, n) for n in widths] + [buf(192, 128)]
+    scratch += [buf(768, n) for n in widths] + [buf(256, 128)]
     scratch += [buf(256, n) for n in widths] + [buf(64, 128)]
     scratch += [buf(1024, 1024) for _ in range(4)] + [buf(512, 1024) for _ in range(4)]
     scratch += [buf(384, 1024) for _ in range(4)]
@@ -710,8 +827,12 @@
     scratch += [buf(1024, 128), buf(1024, 128), buf(1024, 512), buf(1024, 512)]
     scratch += [pltpu.VMEM((2, 1024, 1), F32)] + [buf(512, 128, F32) for _ in range(4)]
     scratch += [buf(128, 1024, F32), buf(128, 1024, F32), buf(16, 1024, F32), buf(128, 128, F32)]
-    scratch += [buf(1, 512, F32)]
+    scratch += [buf(1, 512, F32), buf(64, 384), buf(16, 128), buf(48, 128, F32)]
+    scratch += [pltpu.VMEM((2, 1024, 1), F32), pltpu.VMEM((2, 1024, 1), F32)]
+    scratch += [buf(1024, 128, F32), buf(1024, 128, F32), pltpu.VMEM((2, 1024, 1), F32)]
+    scratch += [buf(1024, 128, F32), buf(1024, 16, F32)]
     scratch += [pltpu.SemaphoreType.DMA((N_SEMS,)), pltpu.SemaphoreType.DMA((N_SEMS,))]
+    scratch += [pltpu.SemaphoreType.DMA((8,))]
     out, gtok, gwi, gwo, gwe, gwc, gsm = pl.pallas_call(
         layer_kernel,
         out_shape=(
@@ -720,18 +841,33 @@
             *(shape((64, n), F32) for n in widths),
             shape((16, 128), F32),
         ),
-        in_specs=[vmem] * 7,
+        in_specs=[pl.BlockSpec(memory_space=pl.ANY)] * 6 + [vmem] * 4,
         out_specs=[vmem] * 7,
         scratch_shapes=scratch,
         compiler_params=pltpu.CompilerParams(
             collective_id=0, has_side_effects=True, vmem_limit_bytes=58 * 1024 * 1024
         ),
-    )(tokens, cotangent, wi, output_proj.T, expand_proj, contract_proj.T, sm)
-    grad_input = jnp.swapaxes(gwi.reshape(64, 3, 128), 0, 1)
-    mine = lax.dynamic_slice(gsm, (0, c * 64), (6, 64))
-    grad_hidden = lax.dynamic_slice(gsm, (6, lax.rem(dp, 4) * 32), (1, 32))
-    grad_head = lax.dynamic_slice(gsm, (7, dp * 8), (2, 8))[:, None, :]
-    return (out, gtok, grad_input, gwo.T, gwe, gwc.T, grad_head, grad_hidden, mine[0:2], mine[2:6])
+    )(
+        tokens, cotangent, input_proj, output_proj.T, expand_proj, contract_proj.T,
+        norm_gains, offsets, hidden_bias, head_bias,
+    )
+    return pl.pallas_call(
+        final_kernel,
+        out_shape=(
+            shape((128, 1024), BF16),
+            shape((128, 1024), F32),
+            shape((3, 64, 128), F32),
+            shape((128, 64), F32),
+            shape((64, 512), F32),
+            shape((512, 64), F32),
+            shape((2, 1, 8), F32),
+            shape((1, 32), F32),
+            shape((2, 64), F32),
+            shape((4, 64), F32),
+        ),
+        in_specs=[vmem] * 7,
+        out_specs=[vmem] * 10,
+    )(out, gtok, gwi, gwo, gwe, gwc, gsm)
 
 
 def solution(mesh):

time: 173 us -> 153 us (0.88)
  Pallas kernels: 157 us -> 147 us
  local copies, waits for them, and re-layouts: 13.7 us -> 4.47 us
    pallas_call x1, Pallas kernels: 157 us -> 144 us  [per_device(): pl.pallas_call(layer_kernel, out_shape=(shape((128, 1024), BF16), shape((...]
    unnamed x24 -> x3, local copies, waits for them, and re-layouts: 7.24 us -> 1.21 us
    dynamic_slice x3 -> x0, local copies, waits for them, and re-layouts: 3.39 us -> none  [the longest x1 1.33 us: per_device(): grad_head = lax.dynamic_slice(gsm, (7, dp * 8), (2, 8))[:, None, :]]
    pallas_call x0 -> x2, local copies, waits for them, and re-layouts: none -> 3.26 us  [per_device(): pl.pallas_call(final_kernel, out_shape=(shape((128, 1024), BF16), shape((...]
    pallas_call x0 -> x1, Pallas kernels: none -> 2.41 us  [per_device(): pl.pallas_call(final_kernel, out_shape=(shape((128, 1024), BF16), shape((...]
where the time goes in v2:
time: 153 us; the launch traced here: 152 us
  Pallas kernels  147 us (96%)
  local copies, waits for them, and re-layouts  4.47 us (3%)
    pallas_call x1, Pallas kernels, per_device(): pl.pallas_call(layer_kernel, out_shape=(shape((128, 1024), BF16), shape((...  144 us
    pallas_call x2, local copies, waits for them, and re-layouts, per_device(): pl.pallas_call(final_kernel, out_shape=(shape((128, 1024), BF16), shape((...  3.26 us

profile of v2, /device:TPU:0, one launch (start us, length us, event | category | flops | bytes accessed | tf_op | source)
XLA Modules:
  0.0 151.8 jit_solution(12259090230408742947)
XLA Ops:
  0.6 0.0 copy-start
  0.7 0.6 copy-done
  1.3 0.6 copy.20.head_ref
  1.9 144.2 %shard_map.177 = (bf16[128,1024]{1,0:T(8,128)(2,1)}, f32[128,1024]{1,0:T(8,128)}, f32[64,384]{1,0:T(8,128)}, f32[64,128]{1,0:T(8,128)}, f32[64,512]{1,0:T(8,128)}, /*index=5*/f32[64,512]{1,0:T(8,128)}, f32[16,128]{1,0:T(8,128)}) custom-call(bf16[128,1024]{1,0:T(8,128)(2,1)} %tok_ref.1, bf16[128,1024]{1,0:T(8,128)(2,1)} %cot_ref.1, ...), custom_call_target="tpu_custom_call" | custom-call | tf_op jit(solution)/shard_map/pallas_call | solution.py:836
  146.1 2.4 %shard_map.178 = (bf16[128,1024]{1,0:T(8,128)(2,1)}, f32[128,1024]{1,0:T(8,128)}, f32[3,64,128]{2,1,0:T(8,128)}, f32[128,64]{1,0:T(8,128)}, f32[64,512]{1,0:T(8,...) custom-call(bf16[128,1024]{1,0:T(8,128)(2,1)} %get-tuple-element.17.o, ...), custom_call_target="tpu_custom_call" | custom-call | tf_op jit(solution)/shard_map/pallas_call | solution.py:854
  148.5 1.5 %copy.21 = f32[128,64]{0,1:T(8,128)} copy(f32[128,64]{1,0:T(8,128)} %get-tuple-element.27) | data formatting | bytes 65536 | tf_op jit(solution)/shard_map/pallas_call | solution.py:854
  150.1 1.7 %copy.22 = f32[512,64]{0,1:T(8,128)} copy(f32[512,64]{1,0:T(8,128)} %get-tuple-element.29) | data formatting | bytes 262144 | tf_op jit(solution)/shard_map/pallas_call | solution.py:854
Async XLA Ops:
  0.6 0.7 copy-start

commit v3 on v2

--- a/solution.py
+++ b/solution.py
@@ -81,10 +81,11 @@
         assert self.sent <= N_SEMS
         return copy
 
-    def send(self, src, dst, recv, to):
+    def send(self, src, dst, recv, to, like=None):
+        sem = self.sent
         copy = self.make(src, dst, recv, to)
         copy.start()
-        self.open.append((None, copy))
+        self.open.append((None, copy) if like is None else (sem, like))
 
     def send_if(self, cond, src, dst, recv, to):
         copy = self.make(src, dst, recv, to)
@@ -107,7 +108,16 @@
 
     def drain(self):
         for cond, copy in self.open:
-            if cond is None:
+            if isinstance(cond, int):
+                pltpu.make_async_remote_copy(
+                    src_ref=copy,
+                    dst_ref=copy,
+                    send_sem=self.send_sems.at[cond],
+                    recv_sem=self.recv_sems.at[0],
+                    device_id={"c": 0},
+                    device_id_type=MESH,
+                ).wait_send()
+            elif cond is None:
                 copy.wait_send()
             else:
                 pl.when(cond)(copy.wait_send)
@@ -133,10 +143,13 @@
     def at(self, pos, part, offset=None):
         return self.buf.at[rows((offset or self.offset)(pos) + part * self.half, self.half)]
 
+    def like(self):
+        return self.buf.at[pl.ds(0, self.half)]
+
     def relay(self, pos, part, slot):
         if self.partner is not None:
             ref = self.at(pos, part)
-            self.ring.links.send(ref, ref, self.pids + slot, self.partner)
+            self.ring.links.send(ref, ref, self.pids + slot, self.partner, self.like())
 
     def start(self):
         r, s = self.ring, self.ring.links.send
@@ -160,20 +173,104 @@
         self.relay(r.right, 1, 5)
 
     def done(self):
+        self.near()
+        self.far()
+        self.own()
+
+    def near(self):
         r, w = self.ring, self.ring.links.wait
         w(self.ids + 1, self.at(r.left, 1), r.to_left)
         self.relay(r.left, 1, 3)
         w(self.ids + 2, self.at(r.right, 0), r.to_right)
         self.relay(r.right, 0, 4)
+        self.relayed(2, ((r.left, 0), (r.left, 1), (r.right, 0), (r.right, 1)))
+
+    def far(self):
+        r, w = self.ring, self.ring.links.wait
         w(self.ids + 4, self.at(r.far, 0), r.to_left)
         self.relay(r.far, 0, 6)
         w(self.ids + 5, self.at(r.far, 1), r.to_right)
         self.relay(r.far, 1, 7)
+        self.relayed(6, ((r.far, 0), (r.far, 1)))
+
+    def own(self):
+        r = self.ring
+        self.relayed(0, ((r.pos, 0), (r.pos, 1)))
+
+    def relayed(self, first, blocks):
         if self.partner is not None:
-            order = ((r.pos, 0), (r.pos, 1), (r.left, 0), (r.left, 1))
-            order += ((r.right, 0), (r.right, 1), (r.far, 0), (r.far, 1))
-            for slot, (pos, part) in enumerate(order):
-                w(self.pids + slot, self.at(pos, part, self.offset_partner), self.partner)
+            for k, (pos, part) in enumerate(blocks):
+                self.ring.links.wait(self.pids + first + k, self.at(pos, part, self.offset_partner), self.partner)
+
+
+class ColumnGather(RingGather):
+    def __init__(self, ring, c, buf, partner):
+        super().__init__(ring, buf, c, buf.shape[0] // 2, partner, 1 - c)
+
+    def at(self, pos, part, core=None):
+        rank = (self.offset if core is None else core) * 4 + pos
+        return self.buf.at[pl.ds(part * self.half, self.half), rows(rank * 128, 128)]
+
+    def like(self):
+        return self.buf.at[pl.ds(0, self.half), pl.ds(0, 128)]
+
+
+class FirstGather(RingGather):
+    def at(self, pos, part, offset=None):
+        return self.buf.at[pos, pl.ds(part * self.half, self.half)]
+
+    def like(self):
+        return self.buf.at[0, pl.ds(0, self.half)]
+
+
+class WeightGatherAlongX:
+    def __init__(self, ring, me, buf, line):
+        self.ring, self.me, self.buf, self.line = ring, me, buf, line
+        self.gather = FirstGather(ring, line, None, line.shape[1] // 2)
+        self.ids = ring.links.slots(4)
+
+    def start_y(self):
+        x, yl, c, yh, z = self.me
+        links = self.ring.links
+        self.gather.done()
+        slot = yl * 2 + c
+        dst = self.buf.at[:, slot]
+        for dl, dh in ((1, 0), (0, 1), (1, 1)):
+            to = {"yl": lax.rem(yl + dl, 2), "yh": lax.rem(yh + dh, 2), "c": yh}
+            links.send(self.line, dst, self.ids + slot, to)
+        links.local_if(c == yh, self.line, dst, self.ids + slot)
+        links.send_if(c != yh, self.line, dst, self.ids + slot, {"c": yh})
+
+    def done(self):
+        for k in range(4):
+            self.ring.links.wait(self.ids + k, self.buf.at[:, k], {"c": 1 - self.me[2]})
+
+
+class Swap:
+    def __init__(self, ring, c, size):
+        self.ring, self.c, self.size = ring, c, size
+        self.rank = c * 4 + ring.pos
+        self.ids = ring.links.slots(8)
+        self.others = [(dc, dz) for dz in (2, 1, 3, 0) for dc in (0, 1) if dc or dz]
+
+    def peer(self, dc, dz):
+        return lax.rem(self.c + dc, 2), lax.rem(self.ring.pos + dz, 4)
+
+    def tile(self, buf, rank):
+        return buf.at[rows(rank * self.size, self.size)]
+
+    def start(self, src, dst):
+        for dc, dz in self.others:
+            to_c, to_z = self.peer(dc, dz)
+            to = {"c": to_c, "z": to_z}
+            self.ring.links.send(self.tile(src, to_c * 4 + to_z), self.tile(dst, self.rank), self.ids + self.rank, to)
+        self.tile(dst, self.rank)[...] = self.tile(src, self.rank)[...]
+
+    def done(self, dst):
+        for dc, dz in self.others:
+            of_c, of_z = self.peer(dc, dz)
+            theirs = of_c * 4 + of_z
+            self.ring.links.wait(self.ids + theirs, self.tile(dst, theirs), {"c": of_c, "z": of_z})
 
 
 class RingSum:
@@ -188,7 +285,8 @@
         return self.land.at[pl.ds(slot * self.half, self.half)]
 
     def send(self, src, slot, to):
-        self.ring.links.send(src, self.landing(slot), self.ids + slot, to)
+        like = self.buf.at[pl.ds(0, self.half)]
+        self.ring.links.send(src, self.landing(slot), self.ids + slot, to, like)
 
     def wait(self, slot, to):
         self.ring.links.wait(self.ids + slot, self.landing(slot), to)
@@ -261,6 +359,30 @@
 
         for pos in range(4):
             self.links.open.append((None, self.core_copy(pos)))
+
+    def run_by_chip(self, body, gather):
+        z = self.order[3]
+
+        @pl.loop(0, 4)
+        def _(i):
+            pl.when(i == 0)(gather.own)
+            pl.when(i == 1)(gather.near)
+
+            @pl.when(i == 3)
+            def _():
+                gather.far()
+                self.core_add(1)
+                self.core_add(2)
+                self.sum.send_near()
+
+            pos = lax.rem(z + jnp.where(i == 2, 3, jnp.where(i == 3, 2, i)), 4)
+            body(pos)
+            self.core_copy(pos).start()
+
+        for pos in range(4):
+            self.links.open.append((None, self.core_copy(pos)))
+        self.core_add(0)
+        self.sum.send_far()
 
     def core_add(self, k):
         got = self.from_core.at[rows(self.order[k] * 128, 128)]
@@ -381,10 +503,10 @@
     out_ref, gtok_ref, gwi_ref, gwo_ref, gwe_ref, gwc_ref, gsm_ref,
     xg, cotg, h1, h2, gbg, wi, wo, we, wc, sm, gi, go, ge, gc, gs,
     land_i, land_o, land_e, land_c, land_s, landy_i, landy_o, landy_e, landy_c, landy_s,
-    part_b, part_o, part_2, part_1, core_b, core_o, core_2, core_1, near_b, near_o, near_2, near_1,
+    part_o, part_2, part_1, core_o, core_2, core_1, near_o, near_2, near_1, wo_all, att_in, gatt_out,
     qkv, gqkv, kvr, gkv_out, gkv_in, att, gatt, hid, gp, lse, dk_acc, dv_acc, dk0_acc, dv0_acc,
     resid, gres, vec, tens, hb_sum, wi_own, sm_own, sm_parts, top, low_sum, att_f, gq_f, delta, columns,
-    vec_t, send_sems, recv_sems, local_sems,
+    vec_t, wq_all, wq_line, send_sems, recv_sems, local_sems,
 ):
     x, yl, c, yh, z = me = tuple(lax.axis_index(a) for a in ("x", "yl", "c", "yh", "z"))
     dp = x * 4 + yl * 2 + c
@@ -417,14 +539,16 @@
             for dh in range(2):
                 if dl or dc:
                     peers.append({"yl": lax.rem(yl + dl, 2), "c": lax.rem(c + dc, 2), "yh": lax.rem(yh + dh, 2)})
+    for dz in (1, 2, 3):
+        peers.append({"c": 1 - c, "z": lax.rem(z + dz, 4)})
     for peer in peers:
         pl.semaphore_signal(barrier, inc=1, device_id=peer, device_id_type=MESH)
     sm_parts[...] = jnp.zeros_like(sm_parts)
     sm_parts[0:2, 0:64] = gain_ref[...].astype(F32)
     sm_parts[2:6, 0:64] = off_ref[...].astype(F32)
     sm_parts[22:23, 0:32] = hid_ref[...].astype(F32)
-    sm_parts[39:40, 0:8] = head_ref[0].astype(F32)
-    sm_parts[40:41, 0:8] = head_ref[1].astype(F32)
+    sm_parts[39:40, 0:8] = head_ref[0:1].astype(F32)
+    sm_parts[40:41, 0:8] = head_ref[1:2].astype(F32)
     placed = pltpu.roll(sm_parts[0:16], c * 64, 1) + pltpu.roll(sm_parts[16:32], lax.rem(dp, 4) * 32, 1)
     sm_own[...] = (placed + pltpu.roll(sm_parts[32:48], dp * 8, 1)).astype(BF16)
     for load in loads:
@@ -432,23 +556,28 @@
     pl.semaphore_wait(barrier, len(peers))
 
     w_sm = WeightGather(ring_x, me, sm, 16, sm_own)
-    w_i = WeightGather(ring_x, me, wi, 64, wi_own)
+    w_kv = WeightGather(ring_x, me, wi.at[:, pl.ds(128, 256)], 64, wi_own.at[:, pl.ds(128, 256)])
+    w_q = WeightGatherAlongX(ring_x, me, wq_all, wq_line)
     w_o = WeightGather(ring_x, me, wo, 64, wo_ref)
     w_e = WeightGather(ring_x, me, we, 64, we_ref)
     w_c = WeightGather(ring_x, me, wc, 64, wc_ref)
     w_sm.start()
-    w_i.start()
+    w_kv.start()
+    wq_line[x] = wi_own[:, 0:128]
+    w_q.gather.start()
     gather_x = RingGather(ring_z, xg, block, 64, partner, block_partner)
     gather_x.start()
     w_o.start()
     w_sm.start_x()
-    w_i.start_x()
-    w_o.start_x()
     w_e.start()
     w_c.start()
+    w_kv.start_x()
+    w_q.gather.forward()
+    w_o.start_x()
     gather_x.forward()
+    w_q.start_y()
     w_sm.gather.forward()
-    w_i.gather.forward()
+    w_kv.gather.forward()
     gather_x.done()
     gather_c = RingGather(ring_z, cotg, block, 64, partner, block_partner)
     gather_c.start()
@@ -471,7 +600,7 @@
         normed, _ = norm_rows(xg[r].astype(F32))
         h1[r] = (normed * gain1 + off0).astype(BF16)
 
-    w_i.gather.done()
+    w_kv.gather.done()
     w_o.gather.forward()
 
     kv_slots = links.slots(2)
@@ -484,13 +613,26 @@
     @pl.loop(0, 4)
     def _(i):
         r = rows(i * 256, 256)
-        qkv[r] = (nn(h1[r], wi[...]) + qkv_bias).astype(BF16)
+        qkv[r, 128:384] = (nn(h1[r], wi[:, 128:384]) + qkv_bias[:, 128:384]).astype(BF16)
         for s in range(2):
             pl.when((i == 2 * s + 1) & (yh == 0))(kv_copies[s].start)
 
+    w_q.done()
+    wi[:, 0:128] = wq_all[...].reshape(1024, 128)
+
+    @pl.loop(0, 4)
+    def _(i):
+        r = rows(i * 256, 256)
+        qkv[r, 0:128] = (nn(h1[r], wi[:, 0:128]) + qkv_bias[:, 0:128]).astype(BF16)
+
+    w_o.gather.done()
     w_e.start_x()
     w_c.start_x()
+    rank = c * 4 + z
+    wo_all[:, rows(rank * 128, 128)] = wo[...]
+    gather_o = ColumnGather(ring_z, c, wo_all, partner)
     gather_c.forward()
+    gather_o.start()
 
     lane = lax.broadcasted_iota(jnp.int32, (1, 128), 1)
     head_lanes = [lane < 64, lane >= 64]
@@ -543,7 +685,8 @@
             att[r] = o.astype(BF16)
 
     attend()
-    w_o.gather.done()
+    gather_o.forward()
+    gather_c.done()
     pl.when(yh == 0)(functools.partial(finish, False))
 
     @pl.when(yh == 1)
@@ -552,19 +695,16 @@
             links.wait(kv_slots + s, kvr.at[pl.ds(s * 512, 512)], {"yh": 0})
         finish(True)
 
-    def branch_tile(r):
-        part_b[r] = nt(att[r], wo[...]).astype(BF16)
-
-    sum_b = GroupSum(ring_z, c, part_b, core_b, near_b)
-    sum_b.run(branch_tile)
-    gather_c.done()
-    sum_b.start()
+    swap_a = Swap(ring_z, c, 128)
+    swap_a.start(att, att_in)
+    x_own = xg[own].astype(F32)
+    cot_own = cotg[own].astype(F32)
     w_e.gather.forward()
     w_c.gather.forward()
-    sum_b.middle()
-    x_own = xg[own].astype(F32)
-    cot_own = cotg[own].astype(F32)
-    resid[...] = x_own + sum_b.total() + off1
+    gather_o.done()
+    swap_a.done(att_in)
+    joined = jnp.concatenate([att_in[128 * k : 128 * k + 128] for k in range(8)], axis=1)
+    resid[...] = x_own + nt(joined, wo_all[...]) + off1
     normed2, inverse2 = norm_rows(resid[...])
     h2[own] = (normed2 * gain2 + off2).astype(BF16)
     gather_h = RingGather(ring_z, h2, block, 64, partner, block_partner)
@@ -573,24 +713,31 @@
     w_c.gather.done()
     vec_t[...] = jnp.transpose(vectors)
     gather_h.forward()
-    gather_h.done()
 
     hb_sum[...] = jnp.zeros_like(hb_sum)
 
-    def mlp_tile(r):
-        p = nn(h2[r], we[...]) + hidden_bias
+    def mlp_tile(pos):
+        near_rows, next_rows = rows(pos * 128, 128), rows(512 + pos * 128, 128)
+
+        def load(ref):
+            return jnp.concatenate([ref[near_rows], ref[next_rows]], axis=0)
+
+        def store(ref, value):
+            ref[near_rows] = value[0:128]
+            ref[next_rows] = value[128:256]
+
+        p = nn(load(h2), we[...]) + hidden_bias
         square = p * p
         t = jnp.tanh(GELU_COEF * (p + CUBIC * p * square))
-        hid[r] = (0.5 * p * (1.0 + t)).astype(BF16)
+        store(hid, (0.5 * p * (1.0 + t)).astype(BF16))
         slope = 0.5 * (1.0 + t) + 0.5 * p * (1.0 - t * t) * (GELU_COEF * (1.0 + 3.0 * CUBIC * square))
-        g = (nn(cotg[r], wc[...]) * slope).astype(BF16)
-        gp[r] = g
+        g = (nn(load(cotg), wc[...]) * slope).astype(BF16)
+        store(gp, g)
         hb_sum[...] += jnp.sum(g.astype(F32), axis=0, keepdims=True)
-        part_2[r] = nt(g, we[...]).astype(BF16)
+        store(part_2, nt(g, we[...]).astype(BF16))
 
     sum_2 = GroupSum(ring_z, c, part_2, core_2, near_2)
-    sum_2.run(mlp_tile)
-    sum_2.start()
+    sum_2.run_by_chip(mlp_tile, gather_h)
 
     def weight_grad(out, left, right):
         @pl.loop(0, 4)
@@ -610,34 +757,36 @@
     gres[...] = cot_own + norm_back(grad2, normed2, inverse2, gain2)
     grad_branch = gres[...].astype(BF16)
     gbg[own] = grad_branch
+    for k in range(4):
+        g = nn(grad_branch, wo_all[:, 256 * k : 256 * k + 256]).astype(BF16)
+        gatt_out[256 * k : 256 * k + 128] = g[:, 0:128]
+        gatt_out[256 * k + 128 : 256 * k + 256] = g[:, 128:256]
+    swap_g = Swap(ring_z, c, 128)
+    swap_g.start(gatt_out, gatt)
     gather_b = RingGather(ring_z, gbg, block, 64, partner, block_partner)
     gather_b.start()
     vec[1:2] = jnp.sum(grad2 * normed2, axis=0, keepdims=True)
     vec[3:4] = jnp.sum(grad_branch.astype(F32), axis=0, keepdims=True)
     vec[4:5] = jnp.sum(grad2, axis=0, keepdims=True)
     vec[5:6] = jnp.sum(cot_own, axis=0, keepdims=True)
-    g_e.middle()
 
     def out_tile(r):
         part_o[r] = nt(hid[r], wc[...]).astype(BF16)
 
     sum_o = GroupSum(ring_z, c, part_o, core_o, near_o)
-    gather_b.forward()
     sum_o.run(out_tile)
-    gather_b.done()
-    sum_o.start()
-    g_c.middle()
+    g_e.middle()
+    swap_g.done(gatt)
 
     @pl.loop(0, 4)
     def _(i):
         r = rows(i * 256, 256)
-        g = nn(gbg[r], wo[...])
-        low = g.astype(BF16)
-        gatt[r] = low
-        product = low.astype(F32) * att_f[r]
+        product = gatt[r].astype(F32) * att_f[r]
         for h in range(2):
             delta[h, r] = jnp.sum(masked(product, h), axis=-1, keepdims=True)
 
+    gather_b.forward()
+    g_c.middle()
     gkv_slots = links.slots(2)
     gkv_copies = []
     for s in range(2):
@@ -702,12 +851,13 @@
 
     pl.when(yh == 1)(attend_far)
     g_e.start_y()
+    sum_o.start()
+    gather_b.done()
+    attend_back()
+    sum_o.middle()
     weight_grad(go, gbg, att)
     g_o = WeightSum(ring_x, me, go, 64, land_o, landy_o)
     g_o.start()
-    attend_back()
-    sum_o.middle()
-    g_o.middle()
 
     @pl.when(yh == 0)
     def _():
@@ -753,10 +903,11 @@
     g_s = SmallSum(ring_x, me, gs, 16, land_s, landy_s)
     g_s.start()
     sum_1.middle()
+    g_o.middle()
     g_c.start_y()
-    g_o.start_y()
     out_ref[...] = (resid[...] + sum_o.total() + off3).astype(BF16)
     g_s.start_y()
+    g_o.start_y()
     g_i.middle()
     normed1, inverse1 = norm_rows(x_own)
     gtok_ref[...] = gres[...] + norm_back(sum_1.total(), normed1, inverse1, gain1)
@@ -795,9 +946,9 @@
     gtok_ref[...] = gtok_k[...]
     for k in range(3):
         gi_ref[k] = gwi[:, 128 * k : 128 * k + 128]
-    go_ref[...] = jnp.transpose(gwo[...])
+    go_ref[...] = gwo[...]
     ge_ref[...] = gwe[...]
-    gc_ref[...] = jnp.transpose(gwc[...])
+    gc_ref[...] = gwc[...]
     small = gsm[...]
     mine = pltpu.roll(small, lax.rem(128 - c * 64, 128), 1)
     gain_ref[...] = mine[0:2, 0:64]
@@ -821,8 +972,9 @@
     scratch += [buf(1024, n) for n in widths] + [buf(256, 128)]
     scratch += [buf(768, n) for n in widths] + [buf(256, 128)]
     scratch += [buf(256, n) for n in widths] + [buf(64, 128)]
-    scratch += [buf(1024, 1024) for _ in range(4)] + [buf(512, 1024) for _ in range(4)]
-    scratch += [buf(384, 1024) for _ in range(4)]
+    scratch += [buf(1024, 1024) for _ in range(3)] + [buf(512, 1024) for _ in range(3)]
+    scratch += [buf(384, 1024) for _ in range(3)]
+    scratch += [buf(1024, 1024), buf(1024, 128), buf(1024, 128)]
     scratch += [buf(1024, 384), buf(1024, 384), buf(1024, 256), buf(1024, 256), buf(1024, 256)]
     scratch += [buf(1024, 128), buf(1024, 128), buf(1024, 512), buf(1024, 512)]
     scratch += [pltpu.VMEM((2, 1024, 1), F32)] + [buf(512, 128, F32) for _ in range(4)]
@@ -831,6 +983,7 @@
     scratch += [pltpu.VMEM((2, 1024, 1), F32), pltpu.VMEM((2, 1024, 1), F32)]
     scratch += [buf(1024, 128, F32), buf(1024, 128, F32), pltpu.VMEM((2, 1024, 1), F32)]
     scratch += [buf(1024, 128, F32), buf(1024, 16, F32)]
+    scratch += [pltpu.VMEM((4, 4, 64, 128), BF16), pltpu.VMEM((4, 64, 128), BF16)]
     scratch += [pltpu.SemaphoreType.DMA((N_SEMS,)), pltpu.SemaphoreType.DMA((N_SEMS,))]
     scratch += [pltpu.SemaphoreType.DMA((8,))]
     out, gtok, gwi, gwo, gwe, gwc, gsm = pl.pallas_call(
@@ -849,17 +1002,17 @@
         ),
     )(
         tokens, cotangent, input_proj, output_proj.T, expand_proj, contract_proj.T,
-        norm_gains, offsets, hidden_bias, head_bias,
+        norm_gains, offsets, hidden_bias, head_bias.reshape(2, 8),
     )
-    return pl.pallas_call(
+    outs = pl.pallas_call(
         final_kernel,
         out_shape=(
             shape((128, 1024), BF16),
             shape((128, 1024), F32),
             shape((3, 64, 128), F32),
-            shape((128, 64), F32),
+            shape((64, 128), F32),
             shape((64, 512), F32),
-            shape((512, 64), F32),
+            shape((64, 512), F32),
             shape((2, 1, 8), F32),
             shape((1, 32), F32),
             shape((2, 64), F32),
@@ -868,6 +1021,7 @@
         in_specs=[vmem] * 7,
         out_specs=[vmem] * 10,
     )(out, gtok, gwi, gwo, gwe, gwc, gsm)
+    return (*outs[:3], outs[3].T, outs[4], outs[5].T, *outs[6:])
 
 
 def solution(mesh):

time: 153 us -> 134 us (0.88)
  Pallas kernels: 147 us -> 132 us
  local copies, waits for them, and re-layouts: 4.47 us -> 0 us
    pallas_call x1, Pallas kernels: 144 us -> 129 us  [per_device(): pl.pallas_call(layer_kernel, out_shape=(shape((128, 1024), BF16), shape((...]
    pallas_call x2 -> x0, local copies, waits for them, and re-layouts: 3.26 us -> none  [per_device(): pl.pallas_call(final_kernel, out_shape=(shape((128, 1024), BF16), shape((...]
where the time goes in v3:
time: 134 us; the launch traced here: 132 us
  Pallas kernels  132 us (99%)
    pallas_call x1, Pallas kernels, per_device(): pl.pallas_call(layer_kernel, out_shape=(shape((128, 1024), BF16), shape((...  129 us

profile of v3, /device:TPU:0, one launch (start us, length us, event | category | flops | bytes accessed | tf_op | source)
XLA Modules:
  0.0 132.4 jit_solution(11314511501309535689)
XLA Ops:
  0.6 129.3 %shard_map.177 = (bf16[128,1024]{1,0:T(8,128)(2,1)}, f32[128,1024]{1,0:T(8,128)}, f32[64,384]{1,0:T(8,128)}, f32[64,128]{1,0:T(8,128)}, f32[64,512]{1,0:T(8,128)}, /*index=5*/f32[64,512]{1,0:T(8,128)}, f32[16,128]{1,0:T(8,128)}) custom-call(bf16[128,1024]{1,0:T(8,128)(2,1)} %tok_ref.1, bf16[128,1024]{1,0:T(8,128)(2,1)} %cot_ref.1, ...), custom_call_target="tpu_custom_call" | custom-call | tf_op jit(solution)/shard_map/pallas_call | solution.py:989
  130.0 2.3 %shard_map.178 = (bf16[128,1024]{1,0:T(8,128)(2,1)}, f32[128,1024]{1,0:T(8,128)}, f32[3,64,128]{2,1,0:T(8,128)}, f32[64,128]{1,0:T(8,128)}, f32[64,512]{1,0:T(8,...) custom-call(bf16[128,1024]{1,0:T(8,128)(2,1)} %get-tuple-element.27.o, ...), custom_call_target="tpu_custom_call" | custom-call | tf_op jit(solution)/shard_map/pallas_call | solution.py:1007

commit v4 on v3

--- a/solution.py
+++ b/solution.py
@@ -17,7 +17,8 @@
 GELU_COEF = 0.7978845608028654
 CUBIC = 0.044715
 SCALE = 64 ** (-0.5)
-N_SEMS = 340
+SENDS = 140
+RECEIVES = 236
 
 
 def nn(a, b):
@@ -54,43 +55,45 @@
 class Links:
     def __init__(self, send_sems, recv_sems):
         self.send_sems, self.recv_sems = send_sems, recv_sems
-        self.sent, self.received, self.open = 0, 0, []
+        self.sent, self.received, self.open, self.free, self.mark = 0, 0, [], [], 0
 
     def outgoing(self, count):
         first = self.sent
         self.sent += count
-        assert self.sent <= N_SEMS
+        assert self.sent <= SENDS, self.sent
         return first
 
     def slots(self, count):
         first = self.received
         self.received += count
-        assert self.received <= N_SEMS
+        assert self.received <= RECEIVES, self.received
         return first
 
     def make(self, src, dst, recv, to):
-        copy = pltpu.make_async_remote_copy(
+        self.last = self.free.pop(0) if self.free else self.outgoing(1)
+        return pltpu.make_async_remote_copy(
             src_ref=src,
             dst_ref=dst,
-            send_sem=self.send_sems.at[self.sent],
+            send_sem=self.send_sems.at[self.last],
             recv_sem=self.recv_sems.at[recv],
             device_id=to,
             device_id_type=MESH,
         )
-        self.sent += 1
-        assert self.sent <= N_SEMS
-        return copy
+
+    def keep(self, copy, cond=None):
+        self.open.append((self.last, cond, copy))
 
     def send(self, src, dst, recv, to, like=None):
-        sem = self.sent
         copy = self.make(src, dst, recv, to)
         copy.start()
-        self.open.append((None, copy) if like is None else (sem, like))
+        if like is not None:
+            copy = like
+        self.keep(copy)
 
     def send_if(self, cond, src, dst, recv, to):
         copy = self.make(src, dst, recv, to)
         pl.when(cond)(copy.start)
-        self.open.append((cond, copy))
+        self.keep(copy, cond)
 
     def local_if(self, cond, src, dst, recv):
         copy = pltpu.make_async_copy(src, dst, self.recv_sems.at[recv])
@@ -106,22 +109,28 @@
             device_id_type=MESH,
         ).wait_recv()
 
-    def drain(self):
-        for cond, copy in self.open:
-            if isinstance(cond, int):
-                pltpu.make_async_remote_copy(
+    def drain(self, count):
+        for sem, cond, copy in self.open[:count]:
+            if not hasattr(copy, "wait_send"):
+                copy = pltpu.make_async_remote_copy(
                     src_ref=copy,
                     dst_ref=copy,
-                    send_sem=self.send_sems.at[cond],
+                    send_sem=self.send_sems.at[sem],
                     recv_sem=self.recv_sems.at[0],
                     device_id={"c": 0},
                     device_id_type=MESH,
-                ).wait_send()
-            elif cond is None:
+                )
+            if cond is None:
                 copy.wait_send()
             else:
                 pl.when(cond)(copy.wait_send)
-        self.open = []
+            if sem is not None:
+                self.free.append(sem)
+        self.open = self.open[count:]
+
+    def settle(self):
+        self.drain(self.mark)
+        self.mark = len(self.open)
 
 
 class Ring:
@@ -358,7 +367,7 @@
                 self.core_copy(tile * 2 + 1).start()
 
         for pos in range(4):
-            self.links.open.append((None, self.core_copy(pos)))
+            self.links.open.append((None, None, self.core_copy(pos)))
 
     def run_by_chip(self, body, gather):
         z = self.order[3]
@@ -380,7 +389,7 @@
             self.core_copy(pos).start()
 
         for pos in range(4):
-            self.links.open.append((None, self.core_copy(pos)))
+            self.links.open.append((None, None, self.core_copy(pos)))
         self.core_add(0)
         self.sum.send_far()
 
@@ -529,18 +538,12 @@
         load.start()
 
     barrier = pltpu.get_barrier_semaphore()
-    peers = [{"x": ring_x.right}, {"x": ring_x.left}, {"x": ring_x.far}]
-    for dh in range(2):
-        for dz in range(4):
-            if dh or dz:
-                peers.append({"yh": lax.rem(yh + dh, 2), "z": lax.rem(z + dz, 4)})
+    peers = [{"x": ring_x.right}, {"x": ring_x.left}, {"z": ring_z.right}, {"z": ring_z.left}]
     for dl in range(2):
         for dc in range(2):
             for dh in range(2):
-                if dl or dc:
+                if dl or dc or dh:
                     peers.append({"yl": lax.rem(yl + dl, 2), "c": lax.rem(c + dc, 2), "yh": lax.rem(yh + dh, 2)})
-    for dz in (1, 2, 3):
-        peers.append({"c": 1 - c, "z": lax.rem(z + dz, 4)})
     for peer in peers:
         pl.semaphore_signal(barrier, inc=1, device_id=peer, device_id_type=MESH)
     sm_parts[...] = jnp.zeros_like(sm_parts)
@@ -600,6 +603,7 @@
         normed, _ = norm_rows(xg[r].astype(F32))
         h1[r] = (normed * gain1 + off0).astype(BF16)
 
+    links.settle()
     w_kv.gather.done()
     w_o.gather.forward()
 
@@ -608,7 +612,7 @@
     for s in range(2):
         part = pl.ds(s * 512, 512)
         kv_copies.append(links.make(qkv.at[part, pl.ds(128, 256)], kvr.at[part], kv_slots + s, {"yh": 1}))
-        links.open.append((yh == 0, kv_copies[s]))
+        links.keep(kv_copies[s], yh == 0)
 
     @pl.loop(0, 4)
     def _(i):
@@ -686,7 +690,7 @@
 
     attend()
     gather_o.forward()
-    gather_c.done()
+    links.settle()
     pl.when(yh == 0)(functools.partial(finish, False))
 
     @pl.when(yh == 1)
@@ -701,6 +705,8 @@
     cot_own = cotg[own].astype(F32)
     w_e.gather.forward()
     w_c.gather.forward()
+    links.settle()
+    gather_c.done()
     gather_o.done()
     swap_a.done(att_in)
     joined = jnp.concatenate([att_in[128 * k : 128 * k + 128] for k in range(8)], axis=1)
@@ -709,6 +715,7 @@
     h2[own] = (normed2 * gain2 + off2).astype(BF16)
     gather_h = RingGather(ring_z, h2, block, 64, partner, block_partner)
     gather_h.start()
+    links.settle()
     w_e.gather.done()
     w_c.gather.done()
     vec_t[...] = jnp.transpose(vectors)
@@ -749,10 +756,12 @@
     g_c = WeightSum(ring_x, me, gc, 64, land_c, landy_c)
     weight_grad(ge, h2, gp)
     g_e.start()
+    links.settle()
     sum_2.middle()
     weight_grad(gc, cotg, hid)
     g_c.start()
 
+    links.settle()
     grad2 = sum_2.total()
     gres[...] = cot_own + norm_back(grad2, normed2, inverse2, gain2)
     grad_branch = gres[...].astype(BF16)
@@ -776,6 +785,7 @@
     sum_o = GroupSum(ring_z, c, part_o, core_o, near_o)
     sum_o.run(out_tile)
     g_e.middle()
+    links.settle()
     swap_g.done(gatt)
 
     @pl.loop(0, 4)
@@ -785,14 +795,12 @@
         for h in range(2):
             delta[h, r] = jnp.sum(masked(product, h), axis=-1, keepdims=True)
 
-    gather_b.forward()
-    g_c.middle()
     gkv_slots = links.slots(2)
     gkv_copies = []
     for s in range(2):
         part = pl.ds(s * 512, 512)
         gkv_copies.append(links.make(gkv_out.at[part], gkv_in.at[part], gkv_slots + s, {"yh": 0}))
-        links.open.append((yh == 1, gkv_copies[s]))
+        links.keep(gkv_copies[s], yh == 1)
 
     def attend_far():
         @pl.loop(0, 2)
@@ -850,6 +858,8 @@
         gq_f[...] = jnp.zeros_like(gq_f)
 
     pl.when(yh == 1)(attend_far)
+    gather_b.forward()
+    g_c.middle()
     g_e.start_y()
     sum_o.start()
     gather_b.done()
@@ -859,6 +869,7 @@
     g_o = WeightSum(ring_x, me, go, 64, land_o, landy_o)
     g_o.start()
 
+    links.settle()
     @pl.when(yh == 0)
     def _():
         for s in range(2):
@@ -869,12 +880,6 @@
                 r = rows(s * 512 + k * 256, 256)
                 gqkv[r, 128:384] = (gqkv[r, 128:384].astype(F32) + gkv_in[r].astype(F32)).astype(BF16)
 
-    def grad1_tile(r):
-        part_1[r] = nt(gqkv[r], wi[...]).astype(BF16)
-
-    sum_1 = GroupSum(ring_z, c, part_1, core_1, near_1)
-    sum_1.run(grad1_tile)
-    sum_1.start()
     head_sums = jnp.sum(gqkv[...].astype(F32), axis=0, keepdims=True)
 
     @pl.loop(0, 4)
@@ -890,6 +895,13 @@
 
     g_i = WeightSum(ring_x, me, gi, 64, land_i, landy_i)
     g_i.start()
+    def grad1_tile(r):
+        part_1[r] = nt(gqkv[r], wi[...]).astype(BF16)
+
+    sum_1 = GroupSum(ring_z, c, part_1, core_1, near_1)
+    sum_1.run(grad1_tile)
+    sum_1.start()
+    g_c.start_y()
     turned = jnp.transpose(columns[...])
     vec[0:1] = turned[0:1]
     vec[2:3] = turned[2:3]
@@ -902,15 +914,16 @@
         gs[pl.ds(16 * k, 16)] = vec[:, 128 * (k // 2) : 128 * (k // 2) + 128].astype(BF16)
     g_s = SmallSum(ring_x, me, gs, 16, land_s, landy_s)
     g_s.start()
+    links.settle()
+    g_i.middle()
+    g_o.middle()
     sum_1.middle()
-    g_o.middle()
-    g_c.start_y()
-    out_ref[...] = (resid[...] + sum_o.total() + off3).astype(BF16)
     g_s.start_y()
+    g_i.start_y()
     g_o.start_y()
-    g_i.middle()
     normed1, inverse1 = norm_rows(x_own)
     gtok_ref[...] = gres[...] + norm_back(sum_1.total(), normed1, inverse1, gain1)
+    links.settle()
     tile = g_s.finish()
     slot = yh * 4 + z
     tens[rows(slot * 16, 16)] = tile
@@ -919,7 +932,7 @@
     others = [(dh, dz) for dh in range(2) for dz in range(4) if dh or dz]
     for dh, dz in others:
         links.send(mine, mine, t_ids + slot, {"yh": lax.rem(yh + dh, 2), "z": lax.rem(z + dz, 4)})
-    g_i.start_y()
+    out_ref[...] = (resid[...] + sum_o.total() + off3).astype(BF16)
     gwe_ref[...] = g_e.finish()
     gwc_ref[...] = g_c.finish()
     gwo_ref[...] = g_o.finish()
@@ -933,7 +946,7 @@
     gsm_ref[0:6] = total[0:6]
     gsm_ref[6:16] = tile[6:16]
     gwi_ref[...] = g_i.finish()
-    links.drain()
+    links.drain(len(links.open))
 
 
 def final_kernel(
@@ -984,8 +997,8 @@
     scratch += [buf(1024, 128, F32), buf(1024, 128, F32), pltpu.VMEM((2, 1024, 1), F32)]
     scratch += [buf(1024, 128, F32), buf(1024, 16, F32)]
     scratch += [pltpu.VMEM((4, 4, 64, 128), BF16), pltpu.VMEM((4, 64, 128), BF16)]
-    scratch += [pltpu.SemaphoreType.DMA((N_SEMS,)), pltpu.SemaphoreType.DMA((N_SEMS,))]
-    scratch += [pltpu.SemaphoreType.DMA((8,))]
+    scratch += [pltpu.SemaphoreType.DMA((SENDS,)), pltpu.SemaphoreType.DMA((RECEIVES,))]
+    scratch += [pltpu.SemaphoreType.DMA((5,))]
     out, gtok, gwi, gwo, gwe, gwc, gsm = pl.pallas_call(
         layer_kernel,
         out_shape=(

time: 134 us -> 125 us (0.933); the launches traced: 132 us -> 125 us
  Pallas kernels: 132 us -> 124 us
    pallas_call x1, Pallas kernels: 129 us -> 122 us  [per_device(): pl.pallas_call(layer_kernel, out_shape=(shape((128, 1024), BF16), shape((...]
where the time goes in v4:
time: 125 us
  Pallas kernels  124 us (99%)
    pallas_call x1, Pallas kernels, per_device(): pl.pallas_call(layer_kernel, out_shape=(shape((128, 1024), BF16), shape((...  122 us

profile of v4, /device:TPU:0, one launch (start us, length us, event | category | flops | bytes accessed | tf_op | source)
XLA Modules:
  0.0 125.1 jit_solution(4980916778590288311)
XLA Ops:
  0.6 122.1 %shard_map.177 = (bf16[128,1024]{1,0:T(8,128)(2,1)}, f32[128,1024]{1,0:T(8,128)}, f32[64,384]{1,0:T(8,128)}, f32[64,128]{1,0:T(8,128)}, f32[64,512]{1,0:T(8,128)}, /*index=5*/f32[64,512]{1,0:T(8,128)}, f32[16,128]{1,0:T(8,128)}) custom-call(bf16[128,1024]{1,0:T(8,128)(2,1)} %tok_ref.1, bf16[128,1024]{1,0:T(8,128)(2,1)} %cot_ref.1, ...), custom_call_target="tpu_custom_call" | custom-call | tf_op jit(solution)/shard_map/pallas_call | solution.py:1002
  122.7 2.3 %shard_map.178 = (bf16[128,1024]{1,0:T(8,128)(2,1)}, f32[128,1024]{1,0:T(8,128)}, f32[3,64,128]{2,1,0:T(8,128)}, f32[64,128]{1,0:T(8,128)}, f32[64,512]{1,0:T(8,...) custom-call(bf16[128,1024]{1,0:T(8,128)(2,1)} %get-tuple-element.27.o, ...), custom_call_target="tpu_custom_call" | custom-call | tf_op jit(solution)/shard_map/pallas_call | solution.py:1020

commit v5 on v4

--- a/solution.py
+++ b/solution.py
@@ -17,7 +17,7 @@
 GELU_COEF = 0.7978845608028654
 CUBIC = 0.044715
 SCALE = 64 ** (-0.5)
-SENDS = 140
+SENDS = 104
 RECEIVES = 236
 
 
@@ -706,7 +706,6 @@
     w_e.gather.forward()
     w_c.gather.forward()
     links.settle()
-    gather_c.done()
     gather_o.done()
     swap_a.done(att_in)
     joined = jnp.concatenate([att_in[128 * k : 128 * k + 128] for k in range(8)], axis=1)
@@ -715,6 +714,7 @@
     h2[own] = (normed2 * gain2 + off2).astype(BF16)
     gather_h = RingGather(ring_z, h2, block, 64, partner, block_partner)
     gather_h.start()
+    gather_c.done()
     links.settle()
     w_e.gather.done()
     w_c.gather.done()

time: 125 us -> 124 us (level)
  no operation moved by 1% of the time
where the time goes in v5:
time: 124 us
  Pallas kernels  123 us (99%)
    pallas_call x1, Pallas kernels, per_device(): pl.pallas_call(layer_kernel, out_shape=(shape((128, 1024), BF16), shape((...  121 us

profile of v5, /device:TPU:0, one launch (start us, length us, event | category | flops | bytes accessed | tf_op | source)
XLA Modules:
  0.0 124.0 jit_solution(12578610950302673543)
XLA Ops:
  0.6 120.9 %shard_map.177 = (bf16[128,1024]{1,0:T(8,128)(2,1)}, f32[128,1024]{1,0:T(8,128)}, f32[64,384]{1,0:T(8,128)}, f32[64,128]{1,0:T(8,128)}, f32[64,512]{1,0:T(8,128)}, /*index=5*/f32[64,512]{1,0:T(8,128)}, f32[16,128]{1,0:T(8,128)}) custom-call(bf16[128,1024]{1,0:T(8,128)(2,1)} %tok_ref.1, bf16[128,1024]{1,0:T(8,128)(2,1)} %cot_ref.1, ...), custom_call_target="tpu_custom_call" | custom-call | tf_op jit(solution)/shard_map/pallas_call | solution.py:1002
  121.6 2.3 %shard_map.178 = (bf16[128,1024]{1,0:T(8,128)(2,1)}, f32[128,1024]{1,0:T(8,128)}, f32[3,64,128]{2,1,0:T(8,128)}, f32[64,128]{1,0:T(8,128)}, f32[64,512]{1,0:T(8,...) custom-call(bf16[128,1024]{1,0:T(8,128)(2,1)} %get-tuple-element.27.o, ...), custom_call_target="tpu_custom_call" | custom-call | tf_op jit(solution)/shard_map/pallas_call | solution.py:1020
